TPU v7x, 128 devices: a whole 4x4x4 slice. The times are simulated.
128 devices in a mesh: dp: 32 (over y, x, core), sub: 4 (over z).
Axes of the slice: x: 4, y: 4, z: 4, core: 2. Of those that a mesh axis runs over, the one named last changes fastest.
Arguments:
- queries: float32 [16384, 4096], P(('dp', 'sub')), may hold values from -1 to 1
- passages: float32 [16384, 4096], P(('dp', 'sub')), may hold values from -1 to 1
- counts: int32 [128, 128], P(('dp', 'sub')), may hold values from 1 to 64, as said below
- hard_owner: int32 [128, 256, 1], P(('dp', 'sub')), may hold values from 0 to 127; in each aligned block of 256 rows (0 to 255, 256 to 511, ..., all dimensions but the last counted through in order) at most 4 rows name the same one
- hard_local: int32 [128, 256], P(('dp', 'sub')), may hold values from 0 to 127
Outputs:
- loss: float32 [], replicated
- query_grad: float32 [16384, 4096], P(('dp', 'sub'))
- passage_grad: float32 [16384, 4096], P(('dp', 'sub'))
Inputs may be any that keep to these rules, and one draw needn't show every extreme that they name: Each row of counts sums to 256, and its largest entry is 64. `hard_owner`: among the 256 slots of one row block at most 4 name the same owner block, and some owner block is named exactly 4 times.
All inputs are finite; a program needn't handle non-finite values.
Results may differ from a plain program's by a relative error of at most 0.0052.
The roundings to bfloat16 on the way count: a program that leaves them out, or rounds other values in their place, can miss the bound.
Values may be sent and summed in bfloat16 or wider, within the bound.
A program may use at most 128 MiB of HBM per device.

v0:
```python
import jax
import jax.numpy as jnp
from jax import lax
from jax.sharding import PartitionSpec as P

sharpness_divisor = 0.02
epsilon = 1e-06


def unit_rows(values):
    norms = jnp.sqrt(jnp.sum(values * values, axis=1, keepdims=True) + epsilon)
    return (values / norms, norms)


def raw_grad(grad, units, norms):
    inner = jnp.sum(units * grad, axis=1, keepdims=True)
    return (grad - units * inner) / norms


def local(queries, passages, counts, hard_owner, hard_local):
    rows = queries.shape[0]
    width = queries.shape[1]
    hard = hard_local.shape[1]
    n_dp = lax.axis_size("dp")
    n_sub = lax.axis_size("sub")
    tiles = n_dp * n_sub
    capacity = max(2, 4 * rows // tiles)
    group = rows * n_sub
    my_sub = lax.axis_index("sub")
    query_dir, query_norm = unit_rows(queries)
    passage_dir, passage_norm = unit_rows(passages)
    query_unit = query_dir.astype(jnp.bfloat16)
    passage_unit = passage_dir.astype(jnp.bfloat16)
    ends = jnp.cumsum(counts[0])
    slots = jnp.arange(hard, dtype=jnp.int32)
    local_query = jnp.sum((ends[None, :] <= slots[:, None]).astype(jnp.int32), axis=1)
    owner = hard_owner[0, :, 0]
    owner_hit = (owner[:, None] == jnp.arange(tiles, dtype=jnp.int32)[None, :]).astype(jnp.int32)
    before = jnp.cumsum(owner_hit, axis=0) - owner_hit
    rank = jnp.sum(before * owner_hit, axis=1)
    place = owner * capacity + rank
    request = jnp.zeros((tiles * capacity,), jnp.int32).at[place].set(hard_local[0])
    wanted = lax.all_to_all(
        request.reshape(tiles, capacity), ("dp", "sub"), split_axis=0, concat_axis=0, tiled=True
    )
    wanted = wanted.reshape(tiles * capacity)
    served = passage_unit[wanted]
    fetched = lax.all_to_all(
        served.reshape(tiles, capacity, width),
        ("dp", "sub"),
        split_axis=0,
        concat_axis=0,
        tiled=True,
    )
    mined_distractor_lines = fetched.reshape(tiles * capacity, width)[place]
    gathered = lax.all_gather(passage_unit, "sub", axis=0, tiled=True)
    batch_scores = (
        lax.dot_general(
            query_unit, gathered, (((1,), (1,)), ((), ())), preferred_element_type=jnp.float32
        )
        / sharpness_divisor
    )
    hard_query_vector = query_unit[local_query]
    mined_cosine_scores = (
        jnp.sum(
            hard_query_vector.astype(jnp.float32) * mined_distractor_lines.astype(jnp.float32),
            axis=1,
        )
        / sharpness_divisor
    )
    exp_batch = jnp.exp(batch_scores)
    exp_hard = jnp.exp(mined_cosine_scores)
    member = local_query[None, :] == jnp.arange(rows, dtype=jnp.int32)[:, None]
    total = jnp.sum(exp_batch, axis=1) + jnp.sum(jnp.where(member, exp_hard[None, :], 0.0), axis=1)
    own_column = my_sub * rows + jnp.arange(rows, dtype=jnp.int32)
    positive_mask = jnp.arange(group, dtype=jnp.int32)[None, :] == own_column[:, None]
    positive = jnp.sum(jnp.where(positive_mask, batch_scores, 0.0), axis=1)
    loss_local = jnp.sum(jnp.log(total) - positive)
    loss = lax.psum(loss_local, ("dp", "sub")) / (rows * tiles)
    inbatch_weighting = (exp_batch / total[:, None] - positive_mask.astype(jnp.float32)).astype(
        jnp.bfloat16
    )
    mined_weighting = (exp_hard / total[local_query]).astype(jnp.bfloat16)
    weight_rows = jnp.where(member, mined_weighting[None, :], jnp.zeros((), jnp.bfloat16))
    query_unit_grad = (
        jnp.dot(inbatch_weighting, gathered, preferred_element_type=jnp.float32)
        + jnp.dot(weight_rows, mined_distractor_lines, preferred_element_type=jnp.float32)
    ) / sharpness_divisor
    position_derivative = (
        mined_weighting.astype(jnp.float32)[:, None]
        * hard_query_vector.astype(jnp.float32)
        / sharpness_divisor
    ).astype(jnp.bfloat16)
    outgoing = jnp.zeros((tiles * capacity, width), jnp.bfloat16).at[place].set(position_derivative)
    returned = lax.all_to_all(
        outgoing.reshape(tiles, capacity, width),
        ("dp", "sub"),
        split_axis=0,
        concat_axis=0,
        tiled=True,
    )
    mined_share = (
        jnp.zeros((rows, width), jnp.float32)
        .at[wanted]
        .add(returned.reshape(tiles * capacity, width).astype(jnp.float32))
    )
    terms = lax.dot_general(
        inbatch_weighting, query_unit, (((0,), (0,)), ((), ())), preferred_element_type=jnp.float32
    )
    inbatch_share = lax.psum_scatter(terms, "sub", scatter_dimension=0, tiled=True)
    unitlength_document_derivative = inbatch_share / sharpness_divisor + mined_share
    return (
        loss,
        raw_grad(query_unit_grad, query_dir, query_norm),
        raw_grad(unitlength_document_derivative, passage_dir, passage_norm),
    )


def solution(mesh):
    in_specs = (
        P(("dp", "sub"), None),
        P(("dp", "sub"), None),
        P(("dp", "sub"), None),
        P(("dp", "sub"), None, None),
        P(("dp", "sub"), None),
    )
    out_specs = (P(), P(("dp", "sub"), None), P(("dp", "sub"), None))
    return jax.shard_map(local, mesh=mesh, in_specs=in_specs, out_specs=out_specs, check_vma=False)
```

profile of v0, /device:TPU:1, one launch (start us, length us, event | category | flops | bytes accessed | tf_op | source)
XLA Modules:
  0.0 306.1 jit_solution(13595721102082129941)
XLA Ops:
  7.2 2.0 multiply_reduce_fusion.2
  12.9 20.9 %all_to_all.19 = s32[128,1,4]{2,1,0:T(1,128)S(1)} all-to-all(s32[128,1,4]{2,1,0:T(1,128)S(1)} %bitcast.34), channel_id=1, replica_groups=mesh['dp'=32,'sub'=4] {'dp','sub'}, dimensions={0} | all-to-all | bytes 4096 | tf_op jit(solution)/shard_map/all_to_all | solution.py:43
  35.3 4.4 %gather_fusion.1 = bf16[512,4096]{1,0:T(8,128)(2,1)} fusion(bf16[128,4096]{1,0:T(8,128)(2,1)S(1)} %copy-done, s32[1024]{0:T(1024)S(1)} %pad_clamp_fusion.1), kind=kCustom, calls=%fused_computation.1 | custom fusion | bytes 8390656 | tf_op jit(solution)/shard_map/gather | solution.py:47
  39.7 7.2 %reshape.183 = bf16[128,4,4096]{2,1,0:T(4,128)(2,1)} reshape(bf16[512,4096]{1,0:T(8,128)(2,1)} %gather_fusion.1) | data formatting | bytes 8388608 | tf_op jit(solution)/shard_map/reshape | solution.py:49
  46.9 5.2 %all-to-all-start.1 = ((bf16[128,4,4096]{2,1,0:T(4,128)(2,1)}), bf16[128,4,4096]{2,1,0:T(4,128)(2,1)}, u32[]{:S(2)}, u32[]{:S(2)}) async-start(bf16[128,4,4096]{2,1,0:T(4,128)(2,1)} %reshape.183), calls=%async_computation.1 | async-start | bytes 8388608 | tf_op jit(solution)/shard_map/all_to_all | solution.py:48
  53.2 1.8 gather_fusion
  55.1 50.0 %all-to-all-done.1 = bf16[128,4,4096]{2,1,0:T(4,128)(2,1)} async-done(((bf16[128,4,4096]{2,1,0:T(4,128)(2,1)}), bf16[128,4,4096]{2,1,0:T(4,128)(2,1)}, u32[]{:S(2)}, u32[]{:S(2)}) %all-to-all-start.1) | async-done | bytes 4194336 | tf_op jit(solution)/shard_map/all_to_all | solution.py:48
  105.1 6.9 %reshape.184 = bf16[512,4096]{1,0:T(8,128)(2,1)} reshape(bf16[128,4,4096]{2,1,0:T(4,128)(2,1)} %all-to-all-done.1) | data formatting | bytes 8388608 | tf_op jit(solution)/shard_map/reshape | solution.py:55
  112.0 7.9 %gather_fusion.2 = bf16[256,4096]{1,0:T(8,128)(2,1)} fusion(bf16[512,4096]{1,0:T(8,128)(2,1)} %reshape.184, s32[1024]{0:T(1024)S(1)} %pad_clamp_fusion), kind=kCustom, calls=%fused_computation.2 | custom fusion | bytes 4195328 | tf_op jit(solution)/shard_map/gather | solution.py:55
  120.0 2.2 fusion.1
  122.3 3.8 %exponential_reduce_fusion = (f32[128]{0:T(128)S(1)}, f32[128]{0:T(128)S(1)}, f32[128,512]{1,0:T(8,128)S(1)}) fusion(s32[128]{0:T(128)S(1)} %iota_add_fusion, bf16[128,4096]{1,0:T(8,128)(2,1)S(1)} %fusion.24, bf16[512,4096]{1,0:T(8,128)(2,1)} %all-gather.2.cloned.1.call-done), kind=kOutput, calls=%fused_computation.32 | convolution fusion | flops 537198336 | bytes 5506560 | tf_op jit(solution)/shard_map/dot_general | solution.py:58
  126.8 4.6 %fusion.22 = f32[512,4096]{1,0:T(8,128)} fusion(bf16[128,4096]{1,0:T(8,128)(2,1)S(1)} %fusion.24, f32[128,512]{1,0:T(8,128)S(1)} %get-tuple-element.9, f32[128]{0:T(128)S(1)} %get-tuple-element.8, s32[128]{0:T(128)S(1)} %iota_add_fusion), kind=kOutput, calls=%fused_computation.66 | convolution fusion | flops 537198592 | bytes 9700352 | tf_op jit(solution)/shard_map/dot_general | solution.py:107
  131.4 1.9 gather_fusion.3
  133.3 6.3 %scatter_custom_fusion.1 = bf16[512,4096]{1,0:T(8,128)(2,1)} fusion(s32[256]{0:T(256)S(1)} %bitcast.43, bf16[256,4096]{1,0:T(8,128)(2,1)S(1)} %gather_fusion, f32[]{:T(128)} %constant.14.clone.1, f32[256]{0:T(256)S(1)} %get-tuple-element.5, bf16[]{:T(256)} %constant.22.clone.1), kind=kCustom, calls=%fused_computation.14 | custom fusion | flops 4194304 | bytes 6292486 | tf_op jit(solution)/shard_map/scatter | solution.py:94
  139.6 7.2 %reshape.185 = bf16[128,4,4096]{2,1,0:T(4,128)(2,1)} reshape(bf16[512,4096]{1,0:T(8,128)(2,1)} %scatter_custom_fusion.1) | data formatting | bytes 8388608 | tf_op jit(solution)/shard_map/reshape | solution.py:96
  146.8 6.4 %all-to-all-start.2 = ((bf16[128,4,4096]{2,1,0:T(4,128)(2,1)}), bf16[128,4,4096]{2,1,0:T(4,128)(2,1)}, u32[]{:S(2)}, u32[]{:S(2)}) async-start(bf16[128,4,4096]{2,1,0:T(4,128)(2,1)} %reshape.185), calls=%async_computation.3 | async-start | bytes 8388608 | tf_op jit(solution)/shard_map/all_to_all | solution.py:95
  153.2 110.0 %psum.7 = f32[]{:T(128)} all-reduce(f32[]{:T(128)} %get-tuple-element.7), channel_id=1, replica_groups=mesh['dp'=32,'sub'=4] {'dp','sub'}, use_global_device_ids=true, to_apply=%region_13.14 | all-reduce | flops 1 | bytes 8 | tf_op jit(solution)/shard_map/psum | solution.py:79
  263.9 3.1 %fusion.23 = f32[128,4096]{1,0:T(8,128)S(1)} fusion(bf16[512,4096]{1,0:T(8,128)(2,1)} %all-gather.2.cloned.1.call-done, f32[128,512]{1,0:T(8,128)S(1)} %get-tuple-element.9, f32[128]{0:T(128)S(1)} %get-tuple-element.8, s32[128]{0:T(128)S(1)} %iota_add_fusion), kind=kOutput, calls=%fused_computation.67 | convolution fusion | flops 537198592 | bytes 6554624 | tf_op jit(solution)/shard_map/dot_general | solution.py:86
  268.2 1.8 subtract_divide_fusion.1
  270.0 7.4 %reshape.239 = f32[512,4096]{1,0:T(8,128)} reshape(bf16[128,4,4096]{2,1,0:T(4,128)(2,1)} %all-to-all-done.2) | data formatting | bytes 12582912 | tf_op jit(solution)/shard_map/convert_element_type | solution.py:105
  277.4 1.8 broadcast_multiply_fusion
  279.1 15.0 %scatter_fusion = f32[128,4096]{1,0:T(8,128)S(1)} fusion(f32[128,4096]{1,0:T(8,128)S(1)} %broadcast_multiply_fusion, s32[512]{0:T(512)S(1)} %bitcast.36, f32[512,4096]{1,0:T(8,128)} %reshape.239), kind=kCustom, calls=%fused_computation.6 | custom fusion | flops 2097152 | bytes 25167872 | tf_op jit(solution)/shard_map/scatter-add | solution.py:105
  294.1 2.1 multiply_reduce_fusion
  296.4 1.8 subtract_divide_fusion
  (58 shorter events, 8.3 us)
Async XLA Ops:
  7.2 2.2 copy-start.1
  7.2 115.2 %all-gather.2.cloned.1.call-start = ((), (), s32[]{:S(2)}) async-start(), calls=%async_computation.4 | async-start | bytes 5242880 | tf_op jit(solution)/shard_map/all_gather | solution.py:56
  9.4 1.2 copy-start.6
  10.6 24.7 %copy-start = (bf16[128,4096]{1,0:T(8,128)(2,1)S(1)}, bf16[128,4096]{1,0:T(8,128)(2,1)}, u32[]{:S(2)}) copy-start(bf16[128,4096]{1,0:T(8,128)(2,1)} %fusion.25) | copy-start | bytes 3145732
  46.9 5.3 %copy-start.7 = (s32[1,128]{1,0:T(1,128)S(1)}, s32[1,128]{1,0:T(1,128)}, u32[]{:S(2)}) copy-start(s32[1,128]{1,0:T(1,128)} %param.7) | copy-start | bytes 1540
  46.9 5.8 %copy-start.3 = (f32[128,4096]{1,0:T(8,128)S(1)}, f32[128,4096]{1,0:T(8,128)}, u32[]{:S(2)}) copy-start(f32[128,4096]{1,0:T(8,128)} %param.5) | copy-start | bytes 6291460
  46.9 58.2 %all-to-all-start.1 = ((bf16[128,4,4096]{2,1,0:T(4,128)(2,1)}), bf16[128,4,4096]{2,1,0:T(4,128)(2,1)}, u32[]{:S(2)}, u32[]{:S(2)}) async-start(bf16[128,4,4096]{2,1,0:T(4,128)(2,1)} %reshape.183), calls=%async_computation.1 | async-start | bytes 8388608 | tf_op jit(solution)/shard_map/all_to_all | solution.py:48
  52.1 225.2 %reduce-scatter.2.cloned.1.call-start = ((), (), s32[]{:S(2)}) async-start(), calls=%async_computation.5 | async-start | bytes 10485760 | tf_op jit(solution)/shard_map/reduce_scatter | solution.py:110
  146.8 123.2 %all-to-all-start.2 = ((bf16[128,4,4096]{2,1,0:T(4,128)(2,1)}), bf16[128,4,4096]{2,1,0:T(4,128)(2,1)}, u32[]{:S(2)}, u32[]{:S(2)}) async-start(bf16[128,4,4096]{2,1,0:T(4,128)(2,1)} %reshape.185), calls=%async_computation.3 | async-start | bytes 8388608 | tf_op jit(solution)/shard_map/all_to_all | solution.py:95
  263.8 3.2 %copy-start.4 = (f32[128,4096]{1,0:T(8,128)S(1)}, f32[128,4096]{1,0:T(8,128)}, u32[]{:S(2)}) copy-start(f32[128,4096]{1,0:T(8,128)} %param.5) | copy-start | bytes 6291460
  263.9 3.5 %copy-start.5 = (bf16[256,4096]{1,0:T(8,128)(2,1)S(1)}, bf16[256,4096]{1,0:T(8,128)(2,1)}, u32[]{:S(2)}) copy-start(bf16[256,4096]{1,0:T(8,128)(2,1)} %gather_fusion.2) | copy-start | bytes 6291460
  294.1 2.2 copy-start.2
Sparse Core Ops, SparseCore 0:
  10.7 98.5 all-gather.1
  131.5 125.0 reduce-scatter.1
where the time goes:
time: 307 us; the launch traced here: 306 us
  blocking collectives  131 us (43%)
  waiting for transfers between devices  50.1 us (16%)
  local copies, waits for them, and re-layouts  47.9 us (16%)
  other arithmetic  37 us (12%)
  between operations  16.1 us (5%)
  matrix products  12.4 us (4%)
  starting transfers between devices  11.7 us (4%)
    psum x1, blocking collectives, local(): loss = lax.psum(loss_local, ('dp', 'sub')) / (rows * tiles)  110 us
    all_to_all x1, waiting for transfers between devices, local(): lax.all_to_all(served.reshape(tiles, capacity, width), ('dp', 'sub'), spl...  50 us
    all_to_all x1, blocking collectives, local(): lax.all_to_all(request.reshape(tiles, capacity), ('dp', 'sub'), split_axi...  20.9 us
    scatter-add x1, other arithmetic, local(): mined_share = jnp.zeros((rows, width), jnp.float32).at[wanted].add(return...  15 us
    gather x1, local copies, waits for them, and re-layouts, local(): mined_distractor_lines = fetched.reshape(tiles * capacity, width)[place]  7.93 us
    convert_element_type x1, local copies, waits for them, and re-layouts, local(): returned.reshape(tiles * capacity, width).astype(jnp.float32)  7.37 us
    reshape x1, local copies, waits for them, and re-layouts, local(): served.reshape(tiles, capacity, width)  7.24 us
    reshape x1, local copies, waits for them, and re-layouts, local(): outgoing.reshape(tiles, capacity, width)  7.2 us
  transfers between devices with their start and end apart: 4, of which 1 were waited for; matrix products, arithmetic and copies ran while one was open for 21% of the time, Pallas kernels for 0%

commit v1 on v0

v1 whole, which is shorter than its diff:
```python
import jax
import jax.numpy as jnp
from jax import lax
from jax.experimental import pallas as pl
from jax.experimental.pallas import tpu as pltpu
from jax.sharding import PartitionSpec as P

MESH = pl.DeviceIdType.MESH
F32 = jnp.float32
BF16 = jnp.bfloat16

sharpness_divisor = 0.02
epsilon = 1e-06

ROWS = 128
WIDTH = 4096
HARD = 256
CAP = 4
N_SUB = 4
N_DP = 32
GROUP = ROWS * N_SUB
SLOTS = N_DP * N_SUB * CAP
MSG = N_SUB * CAP
CHUNKS = 8
CW = WIDTH // CHUNKS


def plane_order():
    def loads(o):
        load = [0, 0, 0, 0]
        for d, axis in ((o[0], 0), (o[1], 2)):
            if d in (1, 2):
                load[axis] += 1
            if d in (3, 2):
                load[axis + 1] += 1
        return load

    rest = [(a, b, c) for a in range(4) for b in range(4) for c in range(2) if (a, b, c) != (0, 0, 0)]
    done, order = [0, 0, 0, 0], []
    while rest:

        def cost(o):
            after = [p + q for p, q in zip(done, loads(o))]
            return (max(after) - min(after), -sum(loads(o)), o[2])

        best = min(rest, key=cost)
        done = [p + q for p, q in zip(done, loads(best))]
        order.append(best)
        rest.remove(best)
    return order


ORDER = plane_order()


def dot(a, b):
    return lax.dot_general(a, b, (((1,), (0,)), ((), ())), preferred_element_type=F32)


def dot_nt(a, b):
    return lax.dot_general(a, b, (((1,), (1,)), ((), ())), preferred_element_type=F32)


def iota(shape, dim):
    return lax.broadcasted_iota(jnp.int32, shape, dim)


def one_hot(mask):
    return jnp.where(mask, 1.0, 0.0).astype(BF16)


def kernel(
    p_hbm, q_hbm, cnt_ref, own_ref, loc_ref,
    loss_ref, qg_hbm, pg_hbm,
    pf, qf, pall, qall, s1, r1, s2, r2,
    e_send, e_recv, f_send, f_recv, cb_send, cb_recv, g_send, g_recv, w_send, w_recv,
    l1_send, l1_recv, l2_send, l2_recv,
    qg, pg, sacc, hacc, es, fs, ftm, chm, cbm, wt, cbt, qinv, pinv,
    in_sem, out_sem, ag_s, ag_r, s1_s, s1_r, s2_s, s2_r, t_s, t_r,
):
    dp = lax.axis_index("dp")
    z = lax.axis_index("sub")
    core = lax.rem(dp, 2)
    x = lax.rem(dp // 2, 4)
    y = dp // 8
    peers = []
    for dx, dy, dc in ORDER:
        peers.append((lax.rem(y + dy, 4) * 4 + lax.rem(x + dx, 4)) * 2 + lax.rem(core + dc, 2))
    mates = [lax.rem(z + d, N_SUB) for d in (1, 3, 2)]

    barrier = pltpu.get_barrier_semaphore()
    for peer in peers:
        pl.semaphore_signal(barrier, inc=1, device_id=(peer, z), device_id_type=MESH)
    for mate in mates:
        pl.semaphore_signal(barrier, inc=1, device_id=(dp, mate), device_id_type=MESH)

    p_in = pltpu.make_async_copy(p_hbm, pf, in_sem.at[0])
    q_in = pltpu.make_async_copy(q_hbm, qf, in_sem.at[1])
    p_in.start()
    q_in.start()

    def rows_at(ref, index, rows):
        return ref.at[pl.ds(pl.multiple_of(index * rows, rows), rows)]

    def landed(ref, rows, sem):
        part = ref.at[pl.ds(0, rows)]
        pltpu.make_async_copy(part, part, sem).wait()

    def to_plane(src, dst, send, recv, rows):
        for peer in peers:
            pltpu.make_async_remote_copy(
                src_ref=rows_at(src, peer, rows), dst_ref=rows_at(dst, dp, rows),
                send_sem=send, recv_sem=recv, device_id=(peer, z), device_id_type=MESH,
            ).start()

    def to_mates(src, dst, send, recv, rows):
        for mate in mates:
            pltpu.make_async_remote_copy(
                src_ref=rows_at(src, mate, rows), dst_ref=rows_at(dst, z, rows),
                send_sem=send, recv_sem=recv, device_id=(dp, mate), device_id_type=MESH,
            ).start()

    def gather_start(buf, k, sem):
        for mate in mates:
            pltpu.make_async_remote_copy(
                src_ref=rows_at(buf.at[k], z, ROWS), dst_ref=rows_at(buf.at[k], z, ROWS),
                send_sem=ag_s.at[sem], recv_sem=ag_r.at[sem],
                device_id=(dp, mate), device_id_type=MESH,
            ).start()

    def keep(src, dst, index, rows):
        at = pl.ds(pl.multiple_of(index * rows, rows), rows)
        dst[at, :] = src[at, :]

    own_row = own_ref[...]
    loc_row = loc_ref[...]
    cnt_row = cnt_ref[...]
    square = (HARD, HARD)
    row_b = jnp.broadcast_to(own_row, square)
    own_col = jnp.sum(jnp.where(iota(square, 0) == iota(square, 1), row_b, 0), axis=1, keepdims=True)
    earlier = (own_col == row_b) & (iota(square, 0) < iota(square, 1))
    rank = jnp.sum(jnp.where(earlier, 1, 0), axis=0, keepdims=True)
    place = own_row * CAP + rank
    slot_at = one_hot(iota((SLOTS, HARD), 0) == place)
    local_t = one_hot(iota((ROWS, HARD), 0) == loc_row)
    cnt_b = jnp.broadcast_to(cnt_row, (ROWS, ROWS))
    upto = iota((ROWS, ROWS), 1) <= iota((ROWS, ROWS), 0)
    before = iota((ROWS, ROWS), 1) < iota((ROWS, ROWS), 0)
    ends = jnp.sum(jnp.where(upto, cnt_b, 0), axis=1, keepdims=True)
    starts = jnp.sum(jnp.where(before, cnt_b, 0), axis=1, keepdims=True)
    slot_id = iota((ROWS, HARD), 1)
    query_t = one_hot((slot_id >= starts) & (slot_id < ends))
    e_send[...] = dot_nt(slot_at, local_t).astype(BF16)
    ftm[...] = dot_nt(query_t, slot_at)
    rz = iota((SLOTS, SLOTS), 0)
    cz = iota((SLOTS, SLOTS), 1)
    by_z = one_hot((rz // ROWS == (cz // CAP) % N_SUB) & ((rz // CAP) % N_DP == cz // MSG) & (rz % CAP == cz % CAP))
    f_send[...] = dot(by_z, dot_nt(slot_at, query_t).astype(BF16)).astype(BF16)

    def normalize(src, inv_ref, dst):
        total = jnp.zeros((ROWS, 1), F32)
        for k in range(CHUNKS):
            v = src[:, k * CW : (k + 1) * CW]
            total += jnp.sum(v * v, axis=1, keepdims=True)
        inv = 1.0 / jnp.sqrt(total + epsilon)
        inv_ref[...] = jnp.broadcast_to(inv, (ROWS, 128))
        at = pl.ds(pl.multiple_of(z * ROWS, ROWS), ROWS)
        for k in range(CHUNKS):
            dst[k, at, :] = (src[:, k * CW : (k + 1) * CW] * inv).astype(BF16)

    p_in.wait()
    normalize(pf, pinv, pall)
    pl.semaphore_wait(barrier, len(peers) + len(mates))
    to_plane(e_send, e_recv, t_s.at[0], t_r.at[0], MSG)
    gather_start(pall, 0, 0)
    gather_start(pall, 1, 1)
    to_mates(f_send, f_recv, t_s.at[1], t_r.at[1], ROWS)
    keep(e_send, e_recv, dp, MSG)
    keep(f_send, f_recv, z, ROWS)
    q_in.wait()
    normalize(qf, qinv, qall)
    sacc[...] = jnp.zeros_like(sacc)
    hacc[...] = jnp.zeros_like(hacc)

    landed(e_recv, SLOTS - MSG, t_r.at[0])
    asked = e_recv[...]
    row_z = (iota((SLOTS, ROWS), 0) // CAP) % N_SUB
    for b in range(N_SUB):
        es[:, b * ROWS : (b + 1) * ROWS] = jnp.where(row_z == b, asked, jnp.zeros_like(asked))

    mine = pl.ds(pl.multiple_of(z * ROWS, ROWS), ROWS)

    def serve_passages(k, carry):
        landed(pall.at[k], GROUP - ROWS, ag_r.at[k])

        @pl.when(k + 2 < CHUNKS)
        def _():
            gather_start(pall, k + 2, k + 2)

        @pl.when(k + 2 >= CHUNKS)
        def _():
            gather_start(qall, k + 2 - CHUNKS, k + 2)

        s1[k] = dot(es[...], pall[k]).astype(BF16)
        to_plane(s1.at[k], r1.at[k], s1_s.at[k], s1_r.at[k], MSG)
        keep(s1.at[k], r1.at[k], dp, MSG)
        sacc[...] += dot_nt(qall[k, mine, :], pall[k])
        return carry

    lax.fori_loop(0, CHUNKS, serve_passages, 0)

    landed(f_recv, GROUP - ROWS, t_r.at[1])
    for b in range(N_SUB):
        ri = iota((SLOTS, ROWS), 0)
        ci = iota((SLOTS, ROWS), 1)
        spread = one_hot((ri // MSG == ci // CAP) & ((ri // CAP) % N_SUB == b) & (ri % CAP == ci % CAP))
        fs[:, b * ROWS : (b + 1) * ROWS] = dot(spread, f_recv[b * ROWS : (b + 1) * ROWS, :]).astype(BF16)

    def serve_queries(k, carry):
        landed(qall.at[k], GROUP - ROWS, ag_r.at[k + CHUNKS])

        @pl.when(k + 2 < CHUNKS)
        def _():
            gather_start(qall, k + 2, k + 2 + CHUNKS)

        s2[k] = dot(fs[...], qall[k]).astype(BF16)
        to_plane(s2.at[k], r2.at[k], s2_s.at[k], s2_r.at[k], MSG)
        keep(s2.at[k], r2.at[k], dp, MSG)
        landed(r1.at[k], SLOTS - MSG, s1_r.at[k])
        hacc[...] += dot_nt(qall[k, mine, :], r1[k])
        return carry

    lax.fori_loop(0, CHUNKS, serve_queries, 0)

    scores = sacc[...] / sharpness_divisor
    exp_batch = jnp.exp(scores)
    exp_hard = jnp.where(ftm[...] > 0.5, jnp.exp(hacc[...] / sharpness_divisor), 0.0)
    total = jnp.sum(exp_batch, axis=1, keepdims=True) + jnp.sum(exp_hard, axis=1, keepdims=True)
    diagonal = iota((ROWS, GROUP), 1) == iota((ROWS, GROUP), 0) + z * ROWS
    positive = jnp.sum(jnp.where(diagonal, scores, 0.0), axis=1, keepdims=True)
    loss_part = jnp.sum(jnp.log(total) - positive, axis=0, keepdims=True)
    l1_send[...] = jnp.broadcast_to(loss_part, (8, 128))
    batch_coef = (exp_batch / total - jnp.where(diagonal, 1.0, 0.0)).astype(BF16)
    hard_coef = (exp_hard / total).astype(BF16)
    cbm[...] = batch_coef
    chm[...] = hard_coef
    for b in range(N_SUB):
        cb_send[b * ROWS : (b + 1) * ROWS, :] = batch_coef[:, b * ROWS : (b + 1) * ROWS]
    spread_coef = lax.dot_general(
        hard_coef, jnp.ones((ROWS, ROWS), BF16), (((0,), (0,)), ((), ())), preferred_element_type=F32
    )
    weighted = (spread_coef * e_send[...].astype(F32)).astype(BF16)
    rz = iota((SLOTS, SLOTS), 0)
    cz = iota((SLOTS, SLOTS), 1)
    by_z = one_hot((rz // ROWS == (cz // CAP) % N_SUB) & ((rz // CAP) % N_DP == cz // MSG) & (rz % CAP == cz % CAP))
    g_send[...] = dot(by_z, weighted).astype(BF16)
    to_mates(g_send, g_recv, t_s.at[2], t_r.at[2], ROWS)
    to_mates(cb_send, cb_recv, t_s.at[3], t_r.at[3], ROWS)
    for mate in mates:
        pltpu.make_async_remote_copy(
            src_ref=l1_send, dst_ref=l1_recv.at[z], send_sem=t_s.at[4], recv_sem=t_r.at[4],
            device_id=(dp, mate), device_id_type=MESH,
        ).start()
    keep(g_send, g_recv, z, ROWS)
    keep(cb_send, cb_recv, z, ROWS)
    l1_recv[z] = l1_send[...]

    landed(g_recv, GROUP - ROWS, t_r.at[2])
    by_dp = one_hot((cz // ROWS == (rz // CAP) % N_SUB) & ((cz // CAP) % N_DP == rz // MSG) & (rz % CAP == cz % CAP))
    w_send[...] = dot(by_dp, g_recv[...]).astype(BF16)
    to_plane(w_send, w_recv, t_s.at[5], t_r.at[5], MSG)
    keep(w_send, w_recv, dp, MSG)
    landed(l1_recv, N_SUB - 1, t_r.at[4])
    l2_send[...] = l1_recv[0] + l1_recv[1] + l1_recv[2] + l1_recv[3]
    for peer in peers:
        pltpu.make_async_remote_copy(
            src_ref=l2_send, dst_ref=l2_recv.at[dp], send_sem=t_s.at[6], recv_sem=t_r.at[6],
            device_id=(peer, z), device_id_type=MESH,
        ).start()
    l2_recv[dp] = l2_send[...]

    scale = 1.0 / sharpness_divisor
    inv = qinv[:, :1]
    inner = jnp.zeros((ROWS, 1), F32)
    for k in range(CHUNKS):
        cols = slice(k * CW, (k + 1) * CW)
        grad = (dot(cbm[...], pall[k]) + dot(chm[...], r1[k])) * scale
        qg[:, cols] = grad
        inner += jnp.sum(qf[:, cols] * inv * grad, axis=1, keepdims=True)
    for k in range(CHUNKS):
        cols = slice(k * CW, (k + 1) * CW)
        qg[:, cols] = (qg[:, cols] - qf[:, cols] * inv * inner) * inv
    q_out = pltpu.make_async_copy(qg, qg_hbm, out_sem.at[0])
    q_out.start()

    landed(cb_recv, GROUP - ROWS, t_r.at[3])
    cbt[...] = jnp.transpose(cb_recv[...].astype(F32)).astype(BF16)
    for k in range(CHUNKS):
        pg[:, k * CW : (k + 1) * CW] = dot(cbt[...], qall[k])
    landed(w_recv, SLOTS - MSG, t_r.at[5])
    wt[...] = jnp.transpose(w_recv[...].astype(F32)).astype(BF16)
    landed(l2_recv, N_DP - 1, t_r.at[6])
    loss_sum = l2_recv[0]
    for d in range(1, N_DP):
        loss_sum = loss_sum + l2_recv[d]
    loss_ref[...] = loss_sum / (ROWS * N_DP * N_SUB)

    inv = pinv[:, :1]
    inner = jnp.zeros((ROWS, 1), F32)
    for k in range(CHUNKS):
        cols = slice(k * CW, (k + 1) * CW)
        landed(r2.at[k], SLOTS - MSG, s2_r.at[k])
        grad = (pg[:, cols] + dot(wt[...], r2[k])) * scale
        pg[:, cols] = grad
        inner += jnp.sum(pf[:, cols] * inv * grad, axis=1, keepdims=True)
    for k in range(CHUNKS):
        cols = slice(k * CW, (k + 1) * CW)
        pg[:, cols] = (pg[:, cols] - pf[:, cols] * inv * inner) * inv
    p_out = pltpu.make_async_copy(pg, pg_hbm, out_sem.at[1])
    p_out.start()

    landed(e_send, SLOTS - MSG, t_s.at[0])
    landed(f_send, GROUP - ROWS, t_s.at[1])
    landed(g_send, GROUP - ROWS, t_s.at[2])
    landed(cb_send, GROUP - ROWS, t_s.at[3])
    landed(l1_recv, N_SUB - 1, t_s.at[4])
    landed(w_send, SLOTS - MSG, t_s.at[5])
    landed(l2_recv, N_DP - 1, t_s.at[6])

    def sent(k, carry):
        landed(pall.at[k], GROUP - ROWS, ag_s.at[k])
        landed(qall.at[k], GROUP - ROWS, ag_s.at[k + CHUNKS])
        landed(s1.at[k], SLOTS - MSG, s1_s.at[k])
        landed(s2.at[k], SLOTS - MSG, s2_s.at[k])
        return carry

    lax.fori_loop(0, CHUNKS, sent, 0)
    q_out.wait()
    p_out.wait()


def local(queries, passages, counts, hard_owner, hard_local):
    vmem = pl.BlockSpec(memory_space=pltpu.VMEM)
    any_space = pl.BlockSpec(memory_space=pl.ANY)
    dma = pltpu.SemaphoreType.DMA
    table = pltpu.VMEM((SLOTS, 128), BF16)
    chunked = pltpu.VMEM((CHUNKS, GROUP, CW), BF16)
    loss, query_grad, passage_grad = pl.pallas_call(
        kernel,
        out_shape=(
            jax.ShapeDtypeStruct((8, 128), F32),
            jax.ShapeDtypeStruct((ROWS, WIDTH), F32),
            jax.ShapeDtypeStruct((ROWS, WIDTH), F32),
        ),
        in_specs=[any_space, any_space, vmem, vmem, vmem],
        out_specs=(vmem, any_space, any_space),
        scratch_shapes=[
            pltpu.VMEM((ROWS, WIDTH), F32), pltpu.VMEM((ROWS, WIDTH), F32),
            chunked, chunked, chunked, chunked, chunked, chunked,
            table, table, table, table, table, table, table, table, table, table,
            pltpu.VMEM((8, 128), F32), pltpu.VMEM((N_SUB, 8, 128), F32),
            pltpu.VMEM((8, 128), F32), pltpu.VMEM((N_DP, 8, 128), F32),
            pltpu.VMEM((ROWS, WIDTH), F32), pltpu.VMEM((ROWS, WIDTH), F32),
            pltpu.VMEM((ROWS, GROUP), F32), pltpu.VMEM((ROWS, SLOTS), F32),
            pltpu.VMEM((SLOTS, GROUP), BF16), pltpu.VMEM((SLOTS, GROUP), BF16),
            pltpu.VMEM((ROWS, SLOTS), F32), pltpu.VMEM((ROWS, SLOTS), BF16), pltpu.VMEM((ROWS, GROUP), BF16),
            pltpu.VMEM((ROWS, SLOTS), BF16), pltpu.VMEM((ROWS, GROUP), BF16),
            pltpu.VMEM((ROWS, 128), F32), pltpu.VMEM((ROWS, 128), F32),
            dma((2,)), dma((2,)), dma((2 * CHUNKS,)), dma((2 * CHUNKS,)),
            dma((CHUNKS,)), dma((CHUNKS,)), dma((CHUNKS,)), dma((CHUNKS,)), dma((7,)), dma((7,)),
        ],
        compiler_params=pltpu.CompilerParams(
            collective_id=0, has_side_effects=True, vmem_limit_bytes=58 * 2**20
        ),
        name="contrastive",
    )(passages, queries, counts, hard_owner.reshape(1, HARD), hard_local)
    return loss[0, 0], query_grad, passage_grad


def solution(mesh):
    in_specs = (
        P(("dp", "sub"), None),
        P(("dp", "sub"), None),
        P(("dp", "sub"), None),
        P(("dp", "sub"), None, None),
        P(("dp", "sub"), None),
    )
    out_specs = (P(), P(("dp", "sub"), None), P(("dp", "sub"), None))
    return jax.shard_map(local, mesh=mesh, in_specs=in_specs, out_specs=out_specs, check_vma=False)
```

time: 307 us -> 127 us (0.41)
  blocking collectives: 131 us -> 0 us
  Pallas kernels: 0 us -> 121 us
  waiting for transfers between devices: 50.1 us -> 0 us
  local copies, waits for them, and re-layouts: 47.9 us -> 5.77 us
  other arithmetic: 37 us -> 0 us
  between operations: 16.1 us -> 0.64 us
  matrix products: 12.4 us -> 0 us
  starting transfers between devices: 11.7 us -> 0 us
    pallas_call x0 -> x1, Pallas kernels: none -> 121 us  [local(): pl.pallas_call(kernel, out_shape=(jax.ShapeDtypeStruct((8, 128), F32), ja...]
    psum x1 -> x0, blocking collectives: 110 us -> none  [local(): loss = lax.psum(loss_local, ('dp', 'sub')) / (rows * tiles)]
    all_to_all x2 -> x0, waiting for transfers between devices: 50 us -> none  [the longest x1 50 us: local(): lax.all_to_all(served.reshape(tiles, capacity, width), ('dp', 'sub'), spl...]
    reshape x4 -> x0, local copies, waits for them, and re-layouts: 21.4 us -> none  [the longest x1 7.24 us: local(): served.reshape(tiles, capacity, width)]
    all_to_all x1 -> x0, blocking collectives: 20.9 us -> none  [local(): lax.all_to_all(request.reshape(tiles, capacity), ('dp', 'sub'), split_axi...]
    gather x4 -> x0, local copies, waits for them, and re-layouts: 16 us -> none  [the longest x1 7.93 us: local(): mined_distractor_lines = fetched.reshape(tiles * capacity, width)[place]]
    scatter-add x1 -> x0, other arithmetic: 15 us -> none  [local(): mined_share = jnp.zeros((rows, width), jnp.float32).at[wanted].add(return...]
    dot_general x4 -> x0, matrix products: 12.4 us -> none  [the longest x1 4.59 us: local(): lax.dot_general(inbatch_weighting, query_unit, (((0,), (0,)), ((), ())),...]
  transfers between devices with their start and end apart: 4 -> 0, of which waited for: 1 -> 0; matrix products, arithmetic and copies ran while one was open for 21% -> 0% of each run, Pallas kernels for 0% -> 0%
where the time goes in v1:
time: 127 us
  Pallas kernels  121 us (95%)
  local copies, waits for them, and re-layouts  5.77 us (5%)
    pallas_call x1, Pallas kernels, local(): pl.pallas_call(kernel, out_shape=(jax.ShapeDtypeStruct((8, 128), F32), ja...  121 us
    unnamed x4, local copies, waits for them, and re-layouts  4.58 us

profile of v1, /device:TPU:1, one launch (start us, length us, event | category | flops | bytes accessed | tf_op | source)
XLA Modules:
  0.0 127.0 jit_solution(15928263204109846780)
XLA Ops:
  0.6 120.6 %contrastive.1 = (f32[8,128]{1,0:T(8,128)}, f32[128,4096]{1,0:T(8,128)}, f32[128,4096]{1,0:T(8,128)}) custom-call(f32[128,4096]{1,0:T(8,128)} %p_hbm.1, f32[128,4096]{1,0:T(8,128)} %q_hbm.1, s32[1,128]{1,0:T(1,128)} %cnt_ref.1, s32[1,256]{1,0:T(1,128)} %bitcast.2, s32[1,256]{1,0:T(1,128)} %loc_ref.1), custom_call_target="tpu_custom_call" | custom-call | tf_op jit(solution)/shard_map/contrastive/pallas_call | solution.py:348
  121.2 1.2 slice.3
  122.4 0.0 copy-start
  122.4 3.3 %copy.10 = f32[128,4096]{1,0:T(8,128)} copy(f32[128,4096]{1,0:T(8,128)} %get-tuple-element.13) | data formatting | bytes 4194304
  125.6 0.0 copy-done
  125.7 1.3 %copy.11 = f32[128,4096]{1,0:T(8,128)} copy(f32[128,4096]{1,0:T(8,128)S(1)} %copy-done) | data formatting | bytes 4194304
Async XLA Ops:
  122.4 3.3 %copy-start = (f32[128,4096]{1,0:T(8,128)S(1)}, f32[128,4096]{1,0:T(8,128)}, u32[]{:S(2)}) copy-start(f32[128,4096]{1,0:T(8,128)} %get-tuple-element.14) | copy-start | bytes 6291460

commit v2 on v1

v2 whole, which is shorter than its diff:
```python
import jax
import jax.numpy as jnp
from jax import lax
from jax.experimental import pallas as pl
from jax.experimental.pallas import tpu as pltpu
from jax.sharding import PartitionSpec as P

MESH = pl.DeviceIdType.MESH
F32 = jnp.float32
BF16 = jnp.bfloat16

sharpness_divisor = 0.02
epsilon = 1e-06

ROWS = 128
WIDTH = 4096
HARD = 256
CAP = 4
N_SUB = 4
N_DP = 32
GROUP = ROWS * N_SUB
SLOTS = N_DP * N_SUB * CAP
MSG = N_SUB * CAP
CHUNKS = 8
CW = WIDTH // CHUNKS
HW = CW // 2
SIDE = 4


def dot(a, b):
    return lax.dot_general(a, b, (((1,), (0,)), ((), ())), preferred_element_type=F32)


def dot_nt(a, b):
    return lax.dot_general(a, b, (((1,), (1,)), ((), ())), preferred_element_type=F32)


def iota(shape, dim):
    return lax.broadcasted_iota(jnp.int32, shape, dim)


def one_hot(mask):
    return jnp.where(mask, 1.0, 0.0).astype(BF16)


def kernel(
    p_hbm, q_hbm, cnt_hbm, own_hbm, loc_hbm,
    loss_ref, qg, pg,
    cnt_ref, own_ref, loc_ref, pf, qf, pall, qall, s1, m1, r1, s2, m2, r2,
    e_send, e_recv, f_send, f_recv, cb_send, cb_recv, g_send, g_recv, w_send, w_recv,
    loss_send, loss_z, loss_x, loss_y, loss_c,
    sacc, hacc, es, fs, ftm, chm, cbm, wt, cbt, qinv, pinv,
    in_sem, sent, ag_r, a_r, b_r, t_s, t_r,
):
    dp = lax.axis_index("dp")
    z = lax.axis_index("sub")
    core = lax.rem(dp, 2)
    x = lax.rem(dp // 2, SIDE)
    y = dp // (2 * SIDE)
    mates = [lax.rem(z + d, N_SUB) for d in (1, 3, 2)]
    mates_x = [lax.rem(x + d, SIDE) for d in (1, 3, 2)]
    mates_y = [lax.rem(y + d, SIDE) for d in (1, 3, 2)]

    def at(x_, y_, c_):
        return ((y_ * SIDE + x_) * 2 + c_, z)

    def each_peer(body):
        def one(i, carry):
            body(lax.rem(dp + i, N_DP))
            return carry

        lax.fori_loop(1, N_DP, one, 0)

    def send(src, dst, send_sem, recv_sem, device):
        pltpu.make_async_remote_copy(
            src_ref=src, dst_ref=dst, send_sem=send_sem, recv_sem=recv_sem,
            device_id=device, device_id_type=MESH,
        ).start()

    def landed(part, sem):
        pltpu.make_async_copy(part, part, sem).wait()

    ints_in = [
        pltpu.make_async_copy(src, dst, in_sem.at[2 + i])
        for i, (src, dst) in enumerate(((cnt_hbm, cnt_ref), (own_hbm, own_ref), (loc_hbm, loc_ref)))
    ]
    p_in = pltpu.make_async_copy(p_hbm, pf, in_sem.at[0])
    q_in = pltpu.make_async_copy(q_hbm, qf, in_sem.at[1])
    for copy in (*ints_in, p_in):
        copy.start()

    barrier = pltpu.get_barrier_semaphore()
    each_peer(lambda peer: pl.semaphore_signal(barrier, inc=1, device_id=(peer, z), device_id_type=MESH))
    for mate in mates:
        pl.semaphore_signal(barrier, inc=1, device_id=(dp, mate), device_id_type=MESH)


    def span(index, rows):
        return pl.ds(pl.multiple_of(index * rows, rows), rows)

    def to_plane(src, dst, sem):
        each_peer(
            lambda peer: send(src.at[span(peer, MSG)], dst.at[span(dp, MSG)], t_s.at[sem], t_r.at[sem], (peer, z))
        )
        dst[span(dp, MSG), :] = src[span(dp, MSG), :]

    def to_mates(src, dst, sem):
        for mate in mates:
            send(src.at[span(mate, ROWS)], dst.at[span(z, ROWS)], t_s.at[sem], t_r.at[sem], (dp, mate))
        dst[span(z, ROWS), :] = src[span(z, ROWS), :]

    def gather_start(buf, k, which):
        mine = buf.at[k, span(z, ROWS)]
        for i in range(2):
            send(mine, mine, sent.at[which], ag_r.at[k, i], (dp, mates[i]))

    def gather_pass_on(buf, k, which):
        for i in range(2):
            landed(buf.at[k, pl.ds(0, ROWS)], ag_r.at[k, i])
            half = ROWS // 2
            part = buf.at[k, pl.ds(pl.multiple_of(mates[1 - i] * ROWS + i * half, half), half)]
            send(part, part, sent.at[which], ag_r.at[k, 2], (dp, mates[i]))

    def gather_done(buf, k):
        landed(buf.at[k, pl.ds(0, ROWS)], ag_r.at[k, 2])

    low, high = pl.ds(0, SIDE), pl.ds(SIDE, SIDE)

    def first_leg(src, mid, k, which):
        for i in range(3):
            send(src.at[k, low, mates_x[i]], mid.at[k, x], sent.at[which], a_r.at[k], at(mates_x[i], y, core))
            send(
                src.at[k, SIDE + mates_y[i]], mid.at[k, SIDE + y], sent.at[which], a_r.at[k], at(x, mates_y[i], core)
            )
        mid[k, x] = src[k, low, x]
        mid[k, SIDE + y] = src[k, SIDE + y]

    def second_leg(mid, dst, k, which):
        mine = span(core, MSG)
        other = span(1 - core, MSG)
        landed(mid.at[k, pl.ds(0, 6)], a_r.at[k])
        done = b_r.at[k + (which - 4) * CHUNKS]

        def pair(x_, y_, part, c):
            send(mid.at[k, low, y_, part], dst.at[k, y, :, mine], sent.at[which], done, at(x, y_, c))
            send(mid.at[k, high, x_, part], dst.at[k, high, x, mine], sent.at[which], done, at(x_, y, c))

        for i in range(3):
            pair(mates_x[i], mates_y[i], mine, core)
            pair(mates_x[i], mates_y[i], other, 1 - core)
        pair(x, y, other, 1 - core)
        dst[k, y, :, mine] = mid[k, low, y, mine]
        dst[k, high, x, mine] = mid[k, high, x, mine]

    def arrived(dst, k, which):
        landed(dst.at[k, pl.ds(0, 7)], b_r.at[k + (which - 4) * CHUNKS])

    def serve(table, buf, dst, k):
        rows = dot(table[...], buf[k]).astype(BF16)
        for h in range(2):
            dst[k, pl.ds(h * SIDE, SIDE)] = rows[:, h * HW : (h + 1) * HW].reshape(SIDE, SIDE, 2 * MSG, HW)

    def rows_of(buf, k, h):
        return buf[k, pl.ds(h * SIDE, SIDE)].reshape(SLOTS, HW)

    with jax.named_scope("integers_in"):
        for copy in ints_in:
            copy.wait()
    own_row = own_ref[...]
    loc_row = loc_ref[...]
    cnt_row = cnt_ref[...]
    square = (HARD, HARD)
    row_b = jnp.broadcast_to(own_row, square)
    own_col = jnp.sum(jnp.where(iota(square, 0) == iota(square, 1), row_b, 0), axis=1, keepdims=True)
    earlier = (own_col == row_b) & (iota(square, 0) < iota(square, 1))
    rank = jnp.sum(jnp.where(earlier, 1, 0), axis=0, keepdims=True)
    place = own_row * CAP + rank
    slot_at = one_hot(iota((SLOTS, HARD), 0) == place)
    local_t = one_hot(iota((ROWS, HARD), 0) == loc_row)
    cnt_b = jnp.broadcast_to(cnt_row, (ROWS, ROWS))
    upto = iota((ROWS, ROWS), 1) <= iota((ROWS, ROWS), 0)
    before = iota((ROWS, ROWS), 1) < iota((ROWS, ROWS), 0)
    ends = jnp.sum(jnp.where(upto, cnt_b, 0), axis=1, keepdims=True)
    starts = jnp.sum(jnp.where(before, cnt_b, 0), axis=1, keepdims=True)
    slot_id = iota((ROWS, HARD), 1)
    query_t = one_hot((slot_id >= starts) & (slot_id < ends))
    e_send[...] = dot_nt(slot_at, local_t).astype(BF16)

    def normalize(src, inv_ref, dst):
        total = jnp.zeros((ROWS, 1), F32)
        for k in range(CHUNKS):
            v = src[:, k * CW : (k + 1) * CW]
            total += jnp.sum(v * v, axis=1, keepdims=True)
        inv = 1.0 / jnp.sqrt(total + epsilon)
        inv_ref[...] = jnp.broadcast_to(inv, (ROWS, 128))
        for k in range(CHUNKS):
            dst[k, span(z, ROWS), :] = (src[:, k * CW : (k + 1) * CW] * inv).astype(BF16)

    with jax.named_scope("entry_barrier"):
        pl.semaphore_wait(barrier, N_DP - 1 + N_SUB - 1)
    to_plane(e_send, e_recv, 0)
    with jax.named_scope("passages_in"):
        p_in.wait()
    q_in.start()
    normalize(pf, pinv, pall)
    gather_start(pall, 0, 0)

    def by_z():
        r, c = iota((SLOTS, SLOTS), 0), iota((SLOTS, SLOTS), 1)
        return one_hot((r // ROWS == (c // CAP) % N_SUB) & ((r // CAP) % N_DP == c // MSG) & (r % CAP == c % CAP))

    def by_dp():
        r, c = iota((SLOTS, SLOTS), 0), iota((SLOTS, SLOTS), 1)
        return one_hot((c // ROWS == (r // CAP) % N_SUB) & ((c // CAP) % N_DP == r // MSG) & (r % CAP == c % CAP))

    ftm[...] = dot_nt(query_t, slot_at)
    f_send[...] = dot(by_z(), dot_nt(slot_at, query_t).astype(BF16)).astype(BF16)
    to_mates(f_send, f_recv, 1)
    q_in.wait()
    normalize(qf, qinv, qall)
    sacc[...] = jnp.zeros_like(sacc)
    hacc[...] = jnp.zeros_like(hacc)

    landed(e_recv.at[pl.ds(0, SLOTS - MSG)], t_r.at[0])
    asked = e_recv[...]
    row_z = (iota((SLOTS, ROWS), 0) // CAP) % N_SUB
    for b in range(N_SUB):
        es[:, b * ROWS : (b + 1) * ROWS] = jnp.where(row_z == b, asked, jnp.zeros_like(asked))

    others = pl.ds(0, GROUP - ROWS)
    gather_pass_on(pall, 0, 0)
    gather_start(pall, 1, 0)
    gather_start(pall, 2, 0)

    def serve_passages(k, carry):
        gather_done(pall, k)
        serve(es, pall, s1, k)
        first_leg(s1, m1, k, 2)

        @pl.when(k + 1 < CHUNKS)
        def _():
            gather_pass_on(pall, k + 1, 0)

        @pl.when(k + 1 == CHUNKS)
        def _():
            gather_pass_on(qall, 0, 1)

        @pl.when(k + 3 < CHUNKS)
        def _():
            gather_start(pall, k + 3, 0)

        @pl.when(k + 3 >= CHUNKS)
        def _():
            gather_start(qall, k + 3 - CHUNKS, 1)

        @pl.when(k > 0)
        def _():
            second_leg(m1, r1, k - 1, 4)

        sacc[...] += dot_nt(qall[k, span(z, ROWS), :], pall[k])
        return carry

    lax.fori_loop(0, CHUNKS, serve_passages, 0)

    landed(f_recv.at[others], t_r.at[1])
    for b in range(N_SUB):
        ri = iota((SLOTS, ROWS), 0)
        ci = iota((SLOTS, ROWS), 1)
        spread = one_hot((ri // MSG == ci // CAP) & ((ri // CAP) % N_SUB == b) & (ri % CAP == ci % CAP))
        fs[:, b * ROWS : (b + 1) * ROWS] = dot(spread, f_recv[b * ROWS : (b + 1) * ROWS, :]).astype(BF16)

    def serve_queries(k, carry):
        gather_done(qall, k)
        serve(fs, qall, s2, k)
        first_leg(s2, m2, k, 3)

        @pl.when(k + 1 < CHUNKS)
        def _():
            gather_pass_on(qall, k + 1, 1)

        @pl.when(k + 3 < CHUNKS)
        def _():
            gather_start(qall, k + 3, 1)

        @pl.when(k == 0)
        def _():
            second_leg(m1, r1, CHUNKS - 1, 4)

        @pl.when(k > 0)
        def _():
            second_leg(m2, r2, k - 1, 5)

        return carry

    def score_hard(k):
        arrived(r1, k, 4)
        for h in range(2):
            hacc[...] += dot_nt(qall[k, span(z, ROWS), h * HW : (h + 1) * HW], rows_of(r1, k, h))

    def serve_and_score(k, carry):
        serve_queries(k, carry)
        score_hard(2 * k)
        score_hard(2 * k + 1)
        return carry

    half = CHUNKS // 2
    lax.fori_loop(0, half, serve_and_score, 0)

    scores = sacc[...] / sharpness_divisor
    exp_batch = jnp.exp(scores)
    exp_hard = jnp.where(ftm[...] > 0.5, jnp.exp(hacc[...] / sharpness_divisor), 0.0)
    total = jnp.sum(exp_batch, axis=1, keepdims=True) + jnp.sum(exp_hard, axis=1, keepdims=True)
    diagonal = iota((ROWS, GROUP), 1) == iota((ROWS, GROUP), 0) + z * ROWS
    positive = jnp.sum(jnp.where(diagonal, scores, 0.0), axis=1, keepdims=True)
    loss_part = jnp.sum(jnp.log(total) - positive, axis=0, keepdims=True)
    loss_send[...] = jnp.broadcast_to(loss_part, (8, 128))
    batch_coef = (exp_batch / total - jnp.where(diagonal, 1.0, 0.0)).astype(BF16)
    hard_coef = (exp_hard / total).astype(BF16)
    cbm[...] = batch_coef
    chm[...] = hard_coef
    for b in range(N_SUB):
        cb_send[b * ROWS : (b + 1) * ROWS, :] = batch_coef[:, b * ROWS : (b + 1) * ROWS]
    spread_coef = lax.dot_general(
        hard_coef, jnp.ones((ROWS, ROWS), BF16), (((0,), (0,)), ((), ())), preferred_element_type=F32
    )
    weighted = (spread_coef * e_send[...].astype(F32)).astype(BF16)
    g_send[...] = dot(by_z(), weighted).astype(BF16)
    to_mates(g_send, g_recv, 2)
    to_mates(cb_send, cb_recv, 3)

    def share_loss(dst, index, sem, devices):
        for device in devices:
            send(loss_send, dst.at[index], t_s.at[sem], t_r.at[sem], device)
        dst[index] = loss_send[...]

    def add_loss(src, sem, count):
        landed(src.at[pl.ds(0, count - 1)], t_r.at[sem])
        landed(src.at[pl.ds(0, count - 1)], t_s.at[sem])
        total = src[0]
        for i in range(1, count):
            total = total + src[i]
        loss_send[...] = total

    share_loss(loss_z, z, 4, [(dp, mate) for mate in mates])

    scale = 1.0 / sharpness_divisor

    def columns(k):
        return pl.ds(pl.multiple_of(k * CW, CW), CW)

    def query_terms(k):
        for h in range(2):
            cols = pl.ds(pl.multiple_of(k * CW + h * HW, HW), HW)
            batch = dot(cbm[...], pall[k, :, h * HW : (h + 1) * HW])
            qg[:, cols] = (batch + dot(chm[...], rows_of(r1, k, h))) * scale

    def serve_and_grad(k, carry):
        serve_queries(k, carry)
        query_terms(2 * k - CHUNKS)
        query_terms(2 * k - CHUNKS + 1)
        return carry

    middle = half + 2
    lax.fori_loop(half, middle, serve_and_grad, 0)

    landed(g_recv.at[others], t_r.at[2])
    w_send[...] = dot(by_dp(), g_recv[...]).astype(BF16)
    to_plane(w_send, w_recv, 5)
    add_loss(loss_z, 4, N_SUB)
    share_loss(loss_x, x, 6, [at(mate, y, core) for mate in mates_x])

    lax.fori_loop(middle, CHUNKS, serve_and_grad, 0)

    landed(cb_recv.at[others], t_r.at[3])
    cbt[...] = jnp.transpose(cb_recv[...].astype(F32)).astype(BF16)
    add_loss(loss_x, 6, SIDE)
    share_loss(loss_y, y, 7, [at(x, mate, core) for mate in mates_y])
    second_leg(m2, r2, CHUNKS - 1, 5)

    inv = qinv[:, :1]
    inner = jnp.zeros((ROWS, 1), F32)
    for k in range(CHUNKS):
        inner += jnp.sum(qf[:, columns(k)] * inv * qg[:, columns(k)], axis=1, keepdims=True)
    for k in range(CHUNKS):
        qg[:, columns(k)] = (qg[:, columns(k)] - qf[:, columns(k)] * inv * inner) * inv

    add_loss(loss_y, 7, SIDE)
    share_loss(loss_c, core, 8, [at(x, y, 1 - core)])
    for k in range(CHUNKS):
        pg[:, columns(k)] = dot(cbt[...], qall[k])
    landed(w_recv.at[pl.ds(0, SLOTS - MSG)], t_r.at[5])
    wt[...] = jnp.transpose(w_recv[...].astype(F32)).astype(BF16)
    add_loss(loss_c, 8, 2)
    loss_ref[...] = loss_send[...] / (ROWS * N_DP * N_SUB)

    inv = pinv[:, :1]
    inner = jnp.zeros((ROWS, 1), F32)
    for k in range(CHUNKS):
        arrived(r2, k, 5)
        for h in range(2):
            cols = slice(k * CW + h * HW, k * CW + (h + 1) * HW)
            grad = (pg[:, cols] + dot(wt[...], rows_of(r2, k, h))) * scale
            pg[:, cols] = grad
            inner += jnp.sum(pf[:, cols] * inv * grad, axis=1, keepdims=True)
    for k in range(CHUNKS):
        pg[:, columns(k)] = (pg[:, columns(k)] - pf[:, columns(k)] * inv * inner) * inv

    landed(e_send.at[pl.ds(0, SLOTS - MSG)], t_s.at[0])
    landed(f_send.at[others], t_s.at[1])
    landed(g_send.at[others], t_s.at[2])
    landed(cb_send.at[others], t_s.at[3])
    landed(w_send.at[pl.ds(0, SLOTS - MSG)], t_s.at[5])
    for i, part in enumerate((pall, qall, m1, m2)):
        landed(part.at[pl.ds(0, 6)], sent.at[i])
    for i, part in enumerate((m1, m2)):
        landed(part.at[pl.ds(0, 7)], sent.at[4 + i])


def write_out(loss_in, q_in, p_in, loss_ref, q_hbm, p_hbm, sem):
    copies = [
        pltpu.make_async_copy(src.at[pl.ds(i * 32, 32)], dst.at[pl.ds(i * 32, 32)], sem.at[j, i])
        for j, (src, dst) in enumerate(((q_in, q_hbm), (p_in, p_hbm)))
        for i in range(4)
    ]
    for copy in copies:
        copy.start()
    loss_ref[0, 0] = loss_in[0, 0]
    for copy in copies:
        copy.wait()


def local(queries, passages, counts, hard_owner, hard_local):
    vmem = pl.BlockSpec(memory_space=pltpu.VMEM)
    any_space = pl.BlockSpec(memory_space=pl.ANY)
    hbm = pl.BlockSpec(memory_space=pltpu.HBM)
    dma = pltpu.SemaphoreType.DMA
    table = pltpu.VMEM((SLOTS, 128), BF16)
    chunked = pltpu.VMEM((CHUNKS, GROUP, CW), BF16)
    routed = pltpu.VMEM((CHUNKS, 2 * SIDE, SIDE, 2 * MSG, HW), BF16)
    grad = pltpu.VMEM((ROWS, WIDTH), F32)
    loss, query_grad, passage_grad = pl.pallas_call(
        kernel,
        out_shape=(pltpu.VMEM((8, 128), F32), grad, grad),
        in_specs=[hbm] * 5,
        out_specs=(vmem, vmem, vmem),
        scratch_shapes=[
            pltpu.VMEM((1, ROWS), jnp.int32), pltpu.VMEM((1, HARD), jnp.int32), pltpu.VMEM((1, HARD), jnp.int32),
            pltpu.VMEM((ROWS, WIDTH), F32), pltpu.VMEM((ROWS, WIDTH), F32),
            chunked, chunked, routed, routed, routed, routed, routed, routed,
            table, table, table, table, table, table, table, table, table, table,
            pltpu.VMEM((8, 128), F32), pltpu.VMEM((N_SUB, 8, 128), F32),
            pltpu.VMEM((SIDE, 8, 128), F32), pltpu.VMEM((SIDE, 8, 128), F32), pltpu.VMEM((2, 8, 128), F32),
            pltpu.VMEM((ROWS, GROUP), F32), pltpu.VMEM((ROWS, SLOTS), F32),
            pltpu.VMEM((SLOTS, GROUP), BF16), pltpu.VMEM((SLOTS, GROUP), BF16),
            pltpu.VMEM((ROWS, SLOTS), F32), pltpu.VMEM((ROWS, SLOTS), BF16), pltpu.VMEM((ROWS, GROUP), BF16),
            pltpu.VMEM((ROWS, SLOTS), BF16), pltpu.VMEM((ROWS, GROUP), BF16),
            pltpu.VMEM((ROWS, 128), F32), pltpu.VMEM((ROWS, 128), F32),
            dma((5,)), dma((6,)), dma((CHUNKS, 3)), dma((CHUNKS,)), dma((2 * CHUNKS,)), dma((9,)), dma((9,)),
        ],
        compiler_params=pltpu.CompilerParams(
            collective_id=0, has_side_effects=True, vmem_limit_bytes=48 * 2**20
        ),
        name="contrastive",
    )(*[
        pltpu.with_memory_space_constraint(v, pltpu.HBM)
        for v in (passages, queries, counts, hard_owner.reshape(1, HARD), hard_local)
    ])
    held = [pltpu.with_memory_space_constraint(v, pltpu.VMEM) for v in (loss, query_grad, passage_grad)]
    loss, query_grad, passage_grad = pl.pallas_call(
        write_out,
        out_shape=(
            jax.ShapeDtypeStruct((1, 1), F32),
            jax.ShapeDtypeStruct((ROWS, WIDTH), F32),
            jax.ShapeDtypeStruct((ROWS, WIDTH), F32),
        ),
        in_specs=[vmem, vmem, vmem],
        out_specs=(pl.BlockSpec(memory_space=pltpu.SMEM), any_space, any_space),
        scratch_shapes=[dma((2, 4))],
        compiler_params=pltpu.CompilerParams(vmem_limit_bytes=8 * 2**20),
        name="write_out",
    )(*held)
    return loss.reshape(()), query_grad, passage_grad


def solution(mesh):
    in_specs = (
        P(("dp", "sub"), None),
        P(("dp", "sub"), None),
        P(("dp", "sub"), None),
        P(("dp", "sub"), None, None),
        P(("dp", "sub"), None),
    )
    out_specs = (P(), P(("dp", "sub"), None), P(("dp", "sub"), None))
    return jax.shard_map(local, mesh=mesh, in_specs=in_specs, out_specs=out_specs, check_vma=False)
```

time: 127 us -> 122 us (0.961)
  local copies, waits for them, and re-layouts: 5.77 us -> 0 us
    unnamed x4 -> x0, local copies, waits for them, and re-layouts: 4.58 us -> none
    pallas_call x1 -> x2, Pallas kernels: 121 us -> 121 us  [the longest x1 119 us: local(): pl.pallas_call(kernel, out_shape=(pltpu.VMEM((8, 128), F32), grad, grad),...]
where the time goes in v2:
time: 122 us
  Pallas kernels  121 us (99%)
    pallas_call x1, Pallas kernels, local(): pl.pallas_call(kernel, out_shape=(pltpu.VMEM((8, 128), F32), grad, grad),...  119 us
    pallas_call x1, Pallas kernels, local(): pl.pallas_call(write_out, out_shape=(jax.ShapeDtypeStruct((1, 1), F32), j...  2.59 us

profile of v2, /device:TPU:1, one launch (start us, length us, event | category | flops | bytes accessed | tf_op | source)
XLA Modules:
  0.0 122.0 jit_solution(10580617116809504409)
XLA Ops:
  0.6 118.8 %contrastive.1 = (f32[8,128]{1,0:T(8,128)S(1)}, f32[128,4096]{1,0:T(8,128)S(1)}, f32[128,4096]{1,0:T(8,128)S(1)}) custom-call(f32[128,4096]{1,0:T(8,128)} %p_hbm.1, f32[128,4096]{1,0:T(8,128)} %q_hbm.1, s32[1,128]{1,0:T(1,128)} %cnt_hbm.1, s32[1,256]{1,0:T(1,128)} %bitcast.2, s32[1,256]{1,0:T(1,128)} %loc_hbm.1), custom_call_target="tpu_custom_call" | custom-call | tf_op jit(solution)/shard_map/contrastive/pallas_call | solution.py:441
  119.5 2.6 %write_out.1 = (f32[1,1]{1,0:T(1,128)}, f32[128,4096]{1,0:T(8,128)}, f32[128,4096]{1,0:T(8,128)}) custom-call(f32[8,128]{1,0:T(8,128)S(1)} %get-tuple-element.9.loss_in, f32[128,4096]{1,0:T(8,128)S(1)} %get-tuple-element.10.q_in, f32[128,4096]{1,0:T(8,128)S(1)} %get-tuple-element.11.p_in), custom_call_target="tpu_custom_call" | custom-call | tf_op jit(solution)/shard_map/write_out/pallas_call | solution.py:469

commit v3 on v2

v3 whole, which is shorter than its diff:
```python
import jax
import jax.numpy as jnp
from jax import lax
from jax.experimental import pallas as pl
from jax.experimental.pallas import tpu as pltpu
from jax.sharding import PartitionSpec as P

MESH = pl.DeviceIdType.MESH
F32 = jnp.float32
BF16 = jnp.bfloat16

sharpness_divisor = 0.02
epsilon = 1e-06

ROWS = 128
WIDTH = 4096
HARD = 256
CAP = 4
N_SUB = 4
N_DP = 32
SIDE = 4
GROUP = ROWS * N_SUB
SLOTS = N_DP * N_SUB * CAP
MSG = N_SUB * CAP
HALVES = 2
SLICES = 4
CW = WIDTH // (HALVES * SLICES)
HW = CW // 2
ITEMS = 16


def dot(a, b):
    return lax.dot_general(a, b, (((1,), (0,)), ((), ())), preferred_element_type=F32)


def dot_nt(a, b):
    return lax.dot_general(a, b, (((1,), (1,)), ((), ())), preferred_element_type=F32)


def iota(shape, dim):
    return lax.broadcasted_iota(jnp.int32, shape, dim)


def one_hot(mask):
    return jnp.where(mask, 1.0, 0.0).astype(BF16)


def columns(a, j):
    start = (j * HALVES + a) * CW
    return slice(start, start + CW)


def block(j):
    return slice(j * ROWS, (j + 1) * ROWS)


def kernel(
    p_hbm, q_hbm, cnt_hbm, own_hbm, loc_hbm,
    loss_ref, qg, pacc, pf, stats,
    cnt_ref, own_ref, loc_ref, qf, pall, qall, sbuf, mbuf, rbuf,
    e_send, e_recv, e_own, f_send, f_recv, cb_send, cb_recv, g_send, g_recv, w_send, w_recv,
    loss_send, loss_z, loss_x, loss_y, loss_c,
    sacc, hacc, es, fs, fk, ft, cbm, cbt, qinv,
    in_sem, sent, ag_r, a_r, b_r, t_s, t_r,
):
    dp = lax.axis_index("dp")
    z = lax.axis_index("sub")
    core = lax.rem(dp, 2)
    x = lax.rem(dp // 2, SIDE)
    y = dp // (2 * SIDE)
    above, below = lax.rem(z + 1, N_SUB), lax.rem(z + 3, N_SUB)
    mates = [(e, lax.rem(z + e, N_SUB)) for e in (1, 3, 2)]
    mates_x = [lax.rem(x + d, SIDE) for d in (1, 3, 2)]
    mates_y = [lax.rem(y + d, SIDE) for d in (1, 3, 2)]

    def at(x_, y_, c_):
        return ((y_ * SIDE + x_) * 2 + c_, z)

    def each_peer(body):
        def one(i, carry):
            body(lax.rem(dp + i, N_DP))
            return carry

        lax.fori_loop(1, N_DP, one, 0)

    def send(src, dst, send_sem, recv_sem, device):
        pltpu.make_async_remote_copy(
            src_ref=src, dst_ref=dst, send_sem=send_sem, recv_sem=recv_sem,
            device_id=device, device_id_type=MESH,
        ).start()

    def landed(part, sem):
        pltpu.make_async_copy(part, part, sem).wait()

    ints_in = [
        pltpu.make_async_copy(src, dst, in_sem.at[2 + i])
        for i, (src, dst) in enumerate(((cnt_hbm, cnt_ref), (own_hbm, own_ref), (loc_hbm, loc_ref)))
    ]
    p_in = pltpu.make_async_copy(p_hbm, pf, in_sem.at[0])
    q_in = pltpu.make_async_copy(q_hbm, qf, in_sem.at[1])
    for copy in (*ints_in, q_in):
        copy.start()

    barrier = pltpu.get_barrier_semaphore()
    each_peer(lambda peer: pl.semaphore_signal(barrier, inc=1, device_id=(peer, z), device_id_type=MESH))
    for _, mate in mates:
        pl.semaphore_signal(barrier, inc=1, device_id=(dp, mate), device_id_type=MESH)

    def span(index, rows):
        return pl.ds(pl.multiple_of(index * rows, rows), rows)

    def to_plane(src, dst, sem):
        each_peer(
            lambda peer: send(src.at[span(peer, MSG)], dst.at[span(dp, MSG)], t_s.at[sem], t_r.at[sem], (peer, z))
        )
        dst[span(dp, MSG), :] = src[span(dp, MSG), :]

    def to_mates(src, dst, sem):
        for e, mate in mates:
            send(
                src.at[pl.ds(e * ROWS, ROWS)], dst.at[pl.ds((N_SUB - e) * ROWS, ROWS)],
                t_s.at[sem], t_r.at[sem], (dp, mate),
            )
        dst[block(0), :] = src[block(0), :]

    def gather_start(buf, a, which):
        send(buf.at[0, a], buf.at[3, a], sent.at[which], ag_r.at[which, a, 0], (dp, above))
        send(buf.at[0, a], buf.at[1, a], sent.at[which], ag_r.at[which, a, 1], (dp, below))

    def gather_pass_on(buf, a, which):
        landed(buf.at[3, a], ag_r.at[which, a, 0])
        upper, lower = pl.ds(0, GROUP // 2), pl.ds(GROUP // 2, GROUP // 2)
        send(buf.at[3, a, upper], buf.at[2, a, upper], sent.at[which], ag_r.at[which, a, 2], (dp, above))
        landed(buf.at[1, a], ag_r.at[which, a, 1])
        send(buf.at[1, a, lower], buf.at[2, a, lower], sent.at[which], ag_r.at[which, a, 2], (dp, below))

    def gather_done(buf, a, which):
        landed(buf.at[2, a], ag_r.at[which, a, 2])

    low, high = pl.ds(0, SIDE), pl.ds(SIDE, SIDE)

    def first_leg(n):
        for i in range(3):
            send(sbuf.at[n, low, mates_x[i]], mbuf.at[n, x], sent.at[2], a_r.at[n], at(mates_x[i], y, core))
            send(sbuf.at[n, SIDE + mates_y[i]], mbuf.at[n, SIDE + y], sent.at[2], a_r.at[n], at(x, mates_y[i], core))
        mbuf[n, x] = sbuf[n, low, x]
        mbuf[n, SIDE + y] = sbuf[n, SIDE + y]

    def second_leg(n):
        mine = span(core, MSG)
        other = span(1 - core, MSG)
        landed(mbuf.at[n, pl.ds(0, 6)], a_r.at[n])

        def pair(x_, y_, part, c):
            send(mbuf.at[n, low, y_, part], rbuf.at[n, y, :, mine], sent.at[3], b_r.at[n], at(x, y_, c))
            send(mbuf.at[n, high, x_, part], rbuf.at[n, high, x, mine], sent.at[3], b_r.at[n], at(x_, y, c))

        for i in range(3):
            pair(mates_x[i], mates_y[i], mine, core)
            pair(mates_x[i], mates_y[i], other, 1 - core)
        pair(x, y, other, 1 - core)
        rbuf[n, y, :, mine] = mbuf[n, low, y, mine]
        rbuf[n, high, x, mine] = mbuf[n, high, x, mine]

    def arrived(n):
        landed(rbuf.at[n, pl.ds(0, 7)], b_r.at[n])

    def serve(n, table, src):
        rows = dot(table, src).astype(BF16)
        for h in range(2):
            sbuf[n, pl.ds(h * SIDE, SIDE)] = rows[:, h * HW : (h + 1) * HW].reshape(SIDE, SIDE, 2 * MSG, HW)

    def rows_of(n):
        parts = [rbuf[n, pl.ds(h * SIDE, SIDE)].reshape(SLOTS, HW) for h in range(2)]
        return jnp.concatenate(parts, axis=1)

    def normalize(src, dst):
        total = jnp.zeros((ROWS, 1), F32)
        for a in range(HALVES):
            for j in range(SLICES):
                v = src[:, columns(a, j)]
                total += jnp.sum(v * v, axis=1, keepdims=True)
        inv = 1.0 / jnp.sqrt(total + epsilon)
        for a in range(HALVES):
            for j in range(SLICES):
                dst[0, a, block(j), :] = (src[:, columns(a, j)] * inv).astype(BF16)
        return jnp.broadcast_to(inv, (ROWS, 128))

    with jax.named_scope("integers_in"):
        for copy in ints_in:
            copy.wait()
    own_row = own_ref[...]
    loc_row = loc_ref[...]
    cnt_row = cnt_ref[...]
    square = (HARD, HARD)
    row_b = jnp.broadcast_to(own_row, square)
    own_col = jnp.sum(jnp.where(iota(square, 0) == iota(square, 1), row_b, 0), axis=1, keepdims=True)
    earlier = (own_col == row_b) & (iota(square, 0) < iota(square, 1))
    rank = jnp.sum(jnp.where(earlier, 1, 0), axis=0, keepdims=True)
    up = (own_row + (N_SUB - z)) % N_SUB
    owner_dp = own_row // N_SUB
    slot_by_up = one_hot(iota((SLOTS, HARD), 0) == up * ROWS + owner_dp * CAP + rank)
    slot_by_dp = one_hot(iota((SLOTS, HARD), 0) == owner_dp * MSG + up * CAP + rank)
    local_t = one_hot(iota((ROWS, HARD), 0) == loc_row)
    cnt_b = jnp.broadcast_to(cnt_row, (ROWS, ROWS))
    upto = iota((ROWS, ROWS), 1) <= iota((ROWS, ROWS), 0)
    before = iota((ROWS, ROWS), 1) < iota((ROWS, ROWS), 0)
    ends = jnp.sum(jnp.where(upto, cnt_b, 0), axis=1, keepdims=True)
    starts = jnp.sum(jnp.where(before, cnt_b, 0), axis=1, keepdims=True)
    slot_id = iota((ROWS, HARD), 1)
    query_t = one_hot((slot_id >= starts) & (slot_id < ends))

    def match(n_dp, n_mid, shape, dim):
        i = iota(shape, dim)
        return i // (n_mid * CAP), (i // CAP) % n_mid, i % CAP

    def spread():
        r = match(N_DP, SLICES, (SLOTS, ROWS), 0)
        c = match(N_DP, 1, (SLOTS, ROWS), 1)
        return one_hot((r[0] == c[0]) & (r[2] == c[2]))

    def spread_t():
        r = match(N_DP, 1, (ROWS, SLOTS), 0)
        c = match(N_DP, SLICES, (ROWS, SLOTS), 1)
        return one_hot((r[0] == c[0]) & (r[2] == c[2]))

    def by_slice(dst, d, rows):
        slice_of = (iota((SLOTS, ROWS), 0) // CAP) % SLICES
        rows = rows.astype(BF16)
        for j in range(SLICES):
            dst[d, :, block(j)] = jnp.where(slice_of == j, rows, jnp.zeros_like(rows))

    def by_slice_t(dst, d, rows):
        slice_of = (iota((ROWS, SLOTS), 1) // CAP) % SLICES
        rows = rows.astype(BF16)
        for j in range(SLICES):
            dst[d, block(j), :] = jnp.where(slice_of == j, rows, jnp.zeros_like(rows))

    f_send[...] = dot_nt(slot_by_up, query_t).astype(BF16)
    by_slice(fs, 0, dot(spread(), f_send[block(0), :]))

    with jax.named_scope("queries_in"):
        q_in.wait()
    p_in.start()
    qinv[...] = normalize(qf, qall)
    serve(0, fs[0], qall[0, 0])
    with jax.named_scope("entry_barrier"):
        pl.semaphore_wait(barrier, N_DP - 1 + N_SUB - 1)
    first_leg(0)
    e_send[...] = dot_nt(slot_by_dp, local_t).astype(BF16)
    to_plane(e_send, e_recv, 0)
    with jax.named_scope("passages_in"):
        p_in.wait()
    stats[0] = normalize(pf, pall)
    gather_start(pall, 0, 0)
    to_mates(f_send, f_recv, 1)
    serve(1, fs[0], qall[0, 1])
    first_leg(1)
    second_leg(0)
    second_leg(1)

    def asked_passages(d):
        r = match(N_DP, SLICES, (SLOTS, SLOTS), 0)
        c = match(N_DP, N_SUB, (SLOTS, SLOTS), 1)
        pick = one_hot((r[0] == c[0]) & (r[2] == c[2]) & (c[1] == d))
        by_slice(es, d, dot(pick, e_recv[...]))

    landed(e_recv.at[pl.ds(0, SLOTS - MSG)], t_r.at[0])
    asked_passages(0)

    def score_batch(d, a):
        part = jnp.zeros((ROWS, ROWS), F32)
        for j in range(SLICES):
            part += dot_nt(qall[0, a, block(j), :], pall[d, a, block(j), :])
        sacc[d] += part

    def score_hard(n, d, a):
        arrived(n)
        pairs = dot_nt(qall[0, a], rows_of(n)) * fk[d].astype(F32)
        hacc[pl.ds(d, 1), :] += jnp.sum(pairs, axis=0, keepdims=True)

    sacc[...] = jnp.zeros_like(sacc)
    hacc[...] = jnp.zeros_like(hacc)
    serve(2, es[0], pall[0, 0])
    first_leg(2)
    e_own[...] = dot_nt(slot_by_up, local_t).astype(BF16)
    for d in range(N_SUB):
        mine = dot_nt(query_t, slot_by_up[block(d), :])
        ft[d] = mine
        by_slice_t(fk, d, dot(mine.astype(BF16), spread_t()))
    gather_pass_on(pall, 0, 0)
    gather_start(pall, 1, 0)
    serve(3, es[0], pall[0, 1])
    first_leg(3)
    second_leg(2)
    for d in range(1, N_SUB):
        asked_passages(d)
    score_batch(0, 0)
    score_batch(0, 1)

    def turn(t):
        i = t % 3
        return 1 + 2 * i - 3 * (i // 2), t // 3, i

    def passages(t, carry):
        d, a, i = turn(t)

        @pl.when(i == 2)
        def _():
            gather_done(pall, a, 0)

        serve(4 + t, es[d], pall[d, a])
        first_leg(4 + t)
        second_leg(3 + t)
        score_batch(d, a)

        @pl.when(t == 2)
        def _():
            gather_pass_on(pall, 1, 0)
            gather_start(qall, 0, 1)

        @pl.when(t == 5)
        def _():
            gather_pass_on(qall, 0, 1)
            gather_start(qall, 1, 1)

        @pl.when((t == 1) | (t == 2))
        def _():
            score_hard(1 + t, 0, t - 1)

        @pl.when(t >= 3)
        def _():
            before_d, before_a, _ = turn(t - 3)
            score_hard(1 + t, before_d, before_a)

        return carry

    lax.fori_loop(0, 6, passages, 0)

    landed(f_recv.at[pl.ds(0, GROUP - ROWS)], t_r.at[1])
    for d in range(1, N_SUB):
        by_slice(fs, d, dot(spread(), f_recv[block(d), :]))

    def queries(t):
        d, a, i = turn(t)
        serve(10 + t, fs[d], qall[d, a])
        first_leg(10 + t)
        second_leg(9 + t)

    def queries_first(t, carry):
        @pl.when(t == 2)
        def _():
            gather_done(qall, 0, 1)

        queries(t)
        before_d, before_a, _ = turn(t + 3)
        score_hard(7 + t, before_d, before_a)
        return carry

    lax.fori_loop(0, 3, queries_first, 0)

    scores = [sacc[d] / sharpness_divisor for d in range(N_SUB)]
    exp_batch = [jnp.exp(v) for v in scores]
    fold = spread().astype(F32)
    hard_scores = (
        lax.dot_general(
            hacc[...], fold, (((1,), (0,)), ((), ())),
            precision=lax.Precision.HIGHEST, preferred_element_type=F32,
        )
        / sharpness_divisor
    )
    used = [jnp.sum(ft[d], axis=0, keepdims=True) for d in range(N_SUB)]
    exp_hard = [jnp.where(used[d] > 0.5, jnp.exp(hard_scores[d : d + 1, :]), 0.0) for d in range(N_SUB)]
    total = jnp.zeros((ROWS, 1), F32)
    for d in range(N_SUB):
        total += jnp.sum(exp_batch[d] + ft[d] * exp_hard[d], axis=1, keepdims=True)
    diagonal = iota((ROWS, ROWS), 1) == iota((ROWS, ROWS), 0)
    positive = jnp.sum(jnp.where(diagonal, scores[0], 0.0), axis=1, keepdims=True)
    loss_part = jnp.sum(jnp.log(total) - positive, axis=0, keepdims=True)
    loss_send[...] = jnp.broadcast_to(loss_part, (8, 128))
    for d in range(N_SUB):
        coef = exp_batch[d] / total
        if d == 0:
            coef = coef - jnp.where(diagonal, 1.0, 0.0)
        cb_send[block(d), :] = coef.astype(BF16)
        cbm[:, block(d)] = coef.astype(BF16)
        slot_total = jnp.sum(ft[d] * total, axis=0, keepdims=True) + (1.0 - used[d])
        hard_coef = (exp_hard[d] / slot_total).astype(BF16)
        hard_row = jnp.broadcast_to(hard_coef.astype(F32), (ROWS, ROWS))
        hard_col = jnp.sum(jnp.where(diagonal, hard_row, 0.0), axis=1, keepdims=True)
        g_send[block(d), :] = (hard_col * e_own[block(d), :].astype(F32)).astype(BF16)
        weight = dot(jnp.broadcast_to(hard_coef, (8, ROWS)), spread_t())[0:1, :]
        fk[d] = (fk[d].astype(F32) * weight).astype(BF16)
    to_mates(g_send, g_recv, 2)
    to_mates(cb_send, cb_recv, 3)

    def share_loss(dst, index, sem, devices):
        for device in devices:
            send(loss_send, dst.at[index], t_s.at[sem], t_r.at[sem], device)
        dst[index] = loss_send[...]

    def add_loss(src, sem, count):
        landed(src.at[pl.ds(0, count - 1)], t_r.at[sem])
        landed(src.at[pl.ds(0, count - 1)], t_s.at[sem])
        added = src[0]
        for i in range(1, count):
            added = added + src[i]
        loss_send[...] = added

    share_loss(loss_z, z, 4, [(dp, mate) for _, mate in mates])

    scale = 1.0 / sharpness_divisor

    def query_terms(a):
        grad = jnp.zeros((GROUP, CW), F32)
        for n, d in ((2 + a, 0), (4 + 3 * a, 1), (5 + 3 * a, 3), (6 + 3 * a, 2)):
            grad += dot(fk[d], rows_of(n))
        for j in range(SLICES):
            batch = dot(cbm[...], pall[:, a, block(j), :].reshape(GROUP, CW))
            qg[:, columns(a, j)] = (grad[block(j), :] + batch) * scale

    gather_pass_on(qall, 1, 1)
    queries(3)
    landed(g_recv.at[pl.ds(0, GROUP - ROWS)], t_r.at[2])
    r = match(N_DP, N_SUB, (SLOTS, SLOTS), 0)
    c = iota((SLOTS, SLOTS), 1)
    by_dp = one_hot((c // ROWS == r[1]) & ((c // CAP) % N_DP == r[0]) & (c % CAP == r[2]))
    w_send[...] = dot(by_dp, g_recv[...]).astype(BF16)
    to_plane(w_send, w_recv, 5)
    add_loss(loss_z, 4, N_SUB)
    share_loss(loss_x, x, 6, [at(mate, y, core) for mate in mates_x])
    query_terms(0)

    queries(4)
    query_terms(1)

    gather_done(qall, 1, 1)
    queries(5)
    add_loss(loss_x, 6, SIDE)
    share_loss(loss_y, y, 7, [at(x, mate, core) for mate in mates_y])

    landed(cb_recv.at[pl.ds(0, GROUP - ROWS)], t_r.at[3])
    cbt[...] = jnp.transpose(cb_recv[...].astype(F32)).astype(BF16)
    for a in range(HALVES):
        for j in range(SLICES):
            pacc[a, block(j), :] = dot(cbt[...], qall[:, a, block(j), :].reshape(GROUP, CW))

    landed(w_recv.at[pl.ds(0, SLOTS - MSG)], t_r.at[5])
    weights_t = jnp.transpose(w_recv[...].astype(F32)).astype(BF16)
    for d in range(N_SUB):
        r = match(N_DP, N_SUB, (SLOTS, SLOTS), 0)
        c = match(N_DP, SLICES, (SLOTS, SLOTS), 1)
        pick = one_hot((r[0] == c[0]) & (r[2] == c[2]) & (r[1] == d))
        by_slice_t(es, d, dot(weights_t, pick))

    def passage_terms(n, d, a):
        arrived(n)
        pacc[a] += dot(es[d], rows_of(n))

    passage_terms(0, 0, 0)
    second_leg(15)
    add_loss(loss_y, 7, SIDE)
    share_loss(loss_c, core, 8, [at(x, y, 1 - core)])
    passage_terms(1, 0, 1)

    inv = qinv[:, :1]
    inner = jnp.zeros((ROWS, 1), F32)
    for a in range(HALVES):
        for j in range(SLICES):
            inner += jnp.sum(qf[:, columns(a, j)] * inv * qg[:, columns(a, j)], axis=1, keepdims=True)
    for a in range(HALVES):
        for j in range(SLICES):
            cols = columns(a, j)
            qg[:, cols] = (qg[:, cols] - qf[:, cols] * inv * inner) * inv

    def more_passage_terms(t, carry):
        d, a, _ = turn(t)
        passage_terms(10 + t, d, a)
        return carry

    inv = stats[0, :, :1]

    def passage_inner(a):
        inner = jnp.zeros((ROWS, 1), F32)
        for j in range(SLICES):
            inner += jnp.sum(pf[:, columns(a, j)] * inv * pacc[a, block(j), :], axis=1, keepdims=True)
        return inner

    lax.fori_loop(0, 3, more_passage_terms, 0)
    first = passage_inner(0)
    add_loss(loss_c, 8, 2)
    loss_ref[...] = loss_send[...] / (ROWS * N_DP * N_SUB)
    lax.fori_loop(3, 6, more_passage_terms, 0)
    stats[1] = jnp.broadcast_to((first + passage_inner(1)) * scale, (ROWS, 128))

    landed(e_send.at[pl.ds(0, SLOTS - MSG)], t_s.at[0])
    landed(f_send.at[pl.ds(0, GROUP - ROWS)], t_s.at[1])
    landed(g_send.at[pl.ds(0, GROUP - ROWS)], t_s.at[2])
    landed(cb_send.at[pl.ds(0, GROUP - ROWS)], t_s.at[3])
    landed(w_send.at[pl.ds(0, SLOTS - MSG)], t_s.at[5])
    landed(pall.at[pl.ds(0, 3)], sent.at[0])
    landed(qall.at[pl.ds(0, 3)], sent.at[1])
    landed(mbuf.at[pl.ds(0, 12)], sent.at[2])
    landed(mbuf.at[pl.ds(0, 14)], sent.at[3])


def write_out(loss_in, q_in, pacc, pf, stats, loss_ref, q_hbm, p_hbm, out, sem):
    copies = [
        pltpu.make_async_copy(q_in.at[pl.ds(i * 32, 32)], q_hbm.at[pl.ds(i * 32, 32)], sem.at[0, i])
        for i in range(4)
    ]
    for copy in copies:
        copy.start()
    loss_ref[0, 0] = loss_in[0, 0]
    scale = 1.0 / sharpness_divisor
    for i in range(4):
        rows = slice(i * 32, (i + 1) * 32)
        inv = stats[0, rows, :1]
        inner = stats[1, rows, :1]
        for a in range(HALVES):
            for j in range(SLICES):
                cols = columns(a, j)
                grad = pacc[a, j * ROWS + i * 32 : j * ROWS + (i + 1) * 32, :] * scale
                out[rows, cols] = (grad - pf[rows, cols] * inv * inner) * inv
        copy = pltpu.make_async_copy(out.at[pl.ds(i * 32, 32)], p_hbm.at[pl.ds(i * 32, 32)], sem.at[1, i])
        copy.start()
        copies.append(copy)
    for copy in copies:
        copy.wait()


def local(queries, passages, counts, hard_owner, hard_local):
    vmem = pl.BlockSpec(memory_space=pltpu.VMEM)
    any_space = pl.BlockSpec(memory_space=pl.ANY)
    hbm = pl.BlockSpec(memory_space=pltpu.HBM)
    dma = pltpu.SemaphoreType.DMA
    table = pltpu.VMEM((SLOTS, 128), BF16)
    gathered = pltpu.VMEM((N_SUB, HALVES, GROUP, CW), BF16)
    routed = pltpu.VMEM((ITEMS, 2 * SIDE, SIDE, 2 * MSG, HW), BF16)
    masks = pltpu.VMEM((N_SUB, SLOTS, GROUP), BF16)
    one_loss = pltpu.VMEM((8, 128), F32)
    rows = pltpu.VMEM((ROWS, WIDTH), F32)
    held = pl.pallas_call(
        kernel,
        out_shape=(
            one_loss, rows, pltpu.VMEM((HALVES, GROUP, CW), F32), rows, pltpu.VMEM((2, ROWS, 128), F32),
        ),
        in_specs=[hbm] * 5,
        out_specs=(vmem,) * 5,
        scratch_shapes=[
            pltpu.VMEM((1, ROWS), jnp.int32), pltpu.VMEM((1, HARD), jnp.int32), pltpu.VMEM((1, HARD), jnp.int32),
            rows, gathered, gathered, routed, routed, routed,
            table, table, table, table, table, table, table, table, table, table, table,
            one_loss, pltpu.VMEM((N_SUB, 8, 128), F32),
            pltpu.VMEM((SIDE, 8, 128), F32), pltpu.VMEM((SIDE, 8, 128), F32), pltpu.VMEM((2, 8, 128), F32),
            pltpu.VMEM((N_SUB, ROWS, ROWS), F32), pltpu.VMEM((8, SLOTS), F32), masks, masks, masks,
            pltpu.VMEM((N_SUB, ROWS, ROWS), F32), pltpu.VMEM((ROWS, GROUP), BF16), pltpu.VMEM((ROWS, GROUP), BF16),
            pltpu.VMEM((ROWS, 128), F32),
            dma((5,)), dma((4,)), dma((2, HALVES, 3)), dma((ITEMS,)), dma((ITEMS,)), dma((9,)), dma((9,)),
        ],
        compiler_params=pltpu.CompilerParams(
            collective_id=0, has_side_effects=True, vmem_limit_bytes=53 * 2**20
        ),
        name="contrastive",
    )(*[
        pltpu.with_memory_space_constraint(v, pltpu.HBM)
        for v in (passages, queries, counts, hard_owner.reshape(1, HARD), hard_local)
    ])
    loss, query_grad, passage_grad = pl.pallas_call(
        write_out,
        out_shape=(
            jax.ShapeDtypeStruct((1, 1), F32),
            jax.ShapeDtypeStruct((ROWS, WIDTH), F32),
            jax.ShapeDtypeStruct((ROWS, WIDTH), F32),
        ),
        in_specs=[vmem] * 5,
        out_specs=(pl.BlockSpec(memory_space=pltpu.SMEM), any_space, any_space),
        scratch_shapes=[rows, dma((2, 4))],
        compiler_params=pltpu.CompilerParams(vmem_limit_bytes=8 * 2**20),
        name="write_out",
    )(*[pltpu.with_memory_space_constraint(v, pltpu.VMEM) for v in held])
    return loss.reshape(()), query_grad, passage_grad


def solution(mesh):
    in_specs = (
        P(("dp", "sub"), None),
        P(("dp", "sub"), None),
        P(("dp", "sub"), None),
        P(("dp", "sub"), None, None),
        P(("dp", "sub"), None),
    )
    out_specs = (P(), P(("dp", "sub"), None), P(("dp", "sub"), None))
    return jax.shard_map(local, mesh=mesh, in_specs=in_specs, out_specs=out_specs, check_vma=False)
```

time: 122 us -> 110 us (0.902)
  Pallas kernels: 121 us -> 109 us
    pallas_call x1, Pallas kernels: 119 us -> 106 us  [local(): pl.pallas_call(kernel, out_shape=(one_loss, rows, pltpu.VMEM((HALVES, GRO...]
where the time goes in v3:
time: 110 us
  Pallas kernels  109 us (99%)
    pallas_call x1, Pallas kernels, local(): pl.pallas_call(kernel, out_shape=(one_loss, rows, pltpu.VMEM((HALVES, GRO...  106 us
    pallas_call x1, Pallas kernels, local(): pl.pallas_call(write_out, out_shape=(jax.ShapeDtypeStruct((1, 1), F32), j...  2.61 us

profile of v3, /device:TPU:1, one launch (start us, length us, event | category | flops | bytes accessed | tf_op | source)
XLA Modules:
  0.0 109.8 jit_solution(5646073692220954124)
XLA Ops:
  0.6 106.4 %contrastive.1 = (f32[8,128]{1,0:T(8,128)S(1)}, f32[128,4096]{1,0:T(8,128)S(1)}, f32[2,512,512]{2,1,0:T(8,128)S(1)}, f32[128,4096]{1,0:T(8,128)S(1)}, f32[2,128,128]{2,1,0:T(8,128)S(1)}) custom-call(f32[128,4096]{1,0:T(8,128)} %p_hbm.1, f32[128,4096]{1,0:T(8,128)} %q_hbm.1, s32[1,128]{1,0:T(1,128)} %cnt_hbm.1, s32[1,256]{1,0:T(1,128)} %bitcast.2, ...), custom_call_target="tpu_custom_call" | custom-call | tf_op jit(solution)/shard_map/contrastive/pallas_call | solution.py:543
  107.0 2.6 %write_out.1 = (f32[1,1]{1,0:T(1,128)}, f32[128,4096]{1,0:T(8,128)}, f32[128,4096]{1,0:T(8,128)}) custom-call(f32[8,128]{1,0:T(8,128)S(1)} %get-tuple-element.11.loss_in, f32[128,4096]{1,0:T(8,128)S(1)} %get-tuple-element.12.q_in, f32[2,512,512]{2,1,0:T(8,128)S(1)} %get-tuple-element.13.pacc, f32[128,4096]{1,0:T(8,128)S(1)} %get-tuple-element.14.pf, ...), custom_call_target="tpu_custom_call" | custom-call | tf_op jit(solution)/shard_map/write_out/pallas_call | solution.py:569

commit v4 on v3

--- a/solution.py
+++ b/solution.py
@@ -58,7 +58,7 @@
     p_hbm, q_hbm, cnt_hbm, own_hbm, loc_hbm,
     loss_ref, qg, pacc, pf, stats,
     cnt_ref, own_ref, loc_ref, qf, pall, qall, sbuf, mbuf, rbuf,
-    e_send, e_recv, e_own, f_send, f_recv, cb_send, cb_recv, g_send, g_recv, w_send, w_recv,
+    e_send, e_recv, f_send, f_recv, cb_send, cb_recv, g_send, g_recv, w_send, w_recv,
     loss_send, loss_z, loss_x, loss_y, loss_c,
     sacc, hacc, es, fs, fk, ft, cbm, cbt, qinv,
     in_sem, sent, ag_r, a_r, b_r, t_s, t_r,
@@ -70,8 +70,8 @@
     y = dp // (2 * SIDE)
     above, below = lax.rem(z + 1, N_SUB), lax.rem(z + 3, N_SUB)
     mates = [(e, lax.rem(z + e, N_SUB)) for e in (1, 3, 2)]
-    mates_x = [lax.rem(x + d, SIDE) for d in (1, 3, 2)]
-    mates_y = [lax.rem(y + d, SIDE) for d in (1, 3, 2)]
+    mates_x = [lax.rem(x + d, SIDE) for d in (2, 1, 3)]
+    mates_y = [lax.rem(y + d, SIDE) for d in (2, 1, 3)]
 
     def at(x_, y_, c_):
         return ((y_ * SIDE + x_) * 2 + c_, z)
@@ -110,10 +110,8 @@
         return pl.ds(pl.multiple_of(index * rows, rows), rows)
 
     def to_plane(src, dst, sem):
-        each_peer(
-            lambda peer: send(src.at[span(peer, MSG)], dst.at[span(dp, MSG)], t_s.at[sem], t_r.at[sem], (peer, z))
-        )
-        dst[span(dp, MSG), :] = src[span(dp, MSG), :]
+        each_peer(lambda peer: send(src.at[peer], dst.at[dp], t_s.at[sem], t_r.at[sem], (peer, z)))
+        dst[dp] = src[dp]
 
     def to_mates(src, dst, sem):
         for e, mate in mates:
@@ -155,9 +153,9 @@
             send(mbuf.at[n, low, y_, part], rbuf.at[n, y, :, mine], sent.at[3], b_r.at[n], at(x, y_, c))
             send(mbuf.at[n, high, x_, part], rbuf.at[n, high, x, mine], sent.at[3], b_r.at[n], at(x_, y, c))
 
-        for i in range(3):
-            pair(mates_x[i], mates_y[i], mine, core)
-            pair(mates_x[i], mates_y[i], other, 1 - core)
+        for part, c in ((other, 1 - core), (mine, core)):
+            for i in range(3):
+                pair(mates_x[i], mates_y[i], part, c)
         pair(x, y, other, 1 - core)
         rbuf[n, y, :, mine] = mbuf[n, low, y, mine]
         rbuf[n, high, x, mine] = mbuf[n, high, x, mine]
@@ -199,9 +197,7 @@
     rank = jnp.sum(jnp.where(earlier, 1, 0), axis=0, keepdims=True)
     up = (own_row + (N_SUB - z)) % N_SUB
     owner_dp = own_row // N_SUB
-    slot_by_up = one_hot(iota((SLOTS, HARD), 0) == up * ROWS + owner_dp * CAP + rank)
-    slot_by_dp = one_hot(iota((SLOTS, HARD), 0) == owner_dp * MSG + up * CAP + rank)
-    local_t = one_hot(iota((ROWS, HARD), 0) == loc_row)
+    slot_at_own = one_hot(iota((ROWS, HARD), 0) == jnp.where(up == 0, owner_dp * CAP + rank, ROWS))
     cnt_b = jnp.broadcast_to(cnt_row, (ROWS, ROWS))
     upto = iota((ROWS, ROWS), 1) <= iota((ROWS, ROWS), 0)
     before = iota((ROWS, ROWS), 1) < iota((ROWS, ROWS), 0)
@@ -236,8 +232,7 @@
         for j in range(SLICES):
             dst[d, block(j), :] = jnp.where(slice_of == j, rows, jnp.zeros_like(rows))
 
-    f_send[...] = dot_nt(slot_by_up, query_t).astype(BF16)
-    by_slice(fs, 0, dot(spread(), f_send[block(0), :]))
+    by_slice(fs, 0, dot(spread(), dot_nt(slot_at_own, query_t).astype(BF16)))
 
     with jax.named_scope("queries_in"):
         q_in.wait()
@@ -247,25 +242,30 @@
     with jax.named_scope("entry_barrier"):
         pl.semaphore_wait(barrier, N_DP - 1 + N_SUB - 1)
     first_leg(0)
-    e_send[...] = dot_nt(slot_by_dp, local_t).astype(BF16)
+    asks = one_hot(iota((N_DP, HARD), 0) == owner_dp)
+    row_at = jnp.where(iota((ROWS, HARD), 0) == up * CAP + rank, loc_row + 1, 0).astype(F32).astype(BF16)
+    e_send[:, 0, :] = dot_nt(asks, row_at)
     to_plane(e_send, e_recv, 0)
     with jax.named_scope("passages_in"):
         p_in.wait()
     stats[0] = normalize(pf, pall)
     gather_start(pall, 0, 0)
-    to_mates(f_send, f_recv, 1)
     serve(1, fs[0], qall[0, 1])
     first_leg(1)
+    slot_by_up = one_hot(iota((SLOTS, HARD), 0) == up * ROWS + owner_dp * CAP + rank)
+    f_send[...] = dot_nt(slot_by_up, query_t).astype(BF16)
+    to_mates(f_send, f_recv, 1)
     second_leg(0)
     second_leg(1)
 
     def asked_passages(d):
-        r = match(N_DP, SLICES, (SLOTS, SLOTS), 0)
-        c = match(N_DP, N_SUB, (SLOTS, SLOTS), 1)
-        pick = one_hot((r[0] == c[0]) & (r[2] == c[2]) & (c[1] == d))
-        by_slice(es, d, dot(pick, e_recv[...]))
-
-    landed(e_recv.at[pl.ds(0, SLOTS - MSG)], t_r.at[0])
+        r = match(N_DP, SLICES, (SLOTS, ROWS), 0)
+        lane = iota((SLOTS, ROWS), 1)
+        asked = dot(one_hot(iota((SLOTS, N_DP), 0) // MSG == iota((SLOTS, N_DP), 1)), e_recv[:, 0, :].astype(BF16))
+        row = jnp.sum(jnp.where(lane == d * CAP + r[2], asked, 0.0), axis=1, keepdims=True)
+        by_slice(es, d, one_hot((lane + 1).astype(F32) == row))
+
+    landed(e_recv.at[pl.ds(0, N_DP - 1)], t_r.at[0])
     asked_passages(0)
 
     def score_batch(d, a):
@@ -283,15 +283,14 @@
     hacc[...] = jnp.zeros_like(hacc)
     serve(2, es[0], pall[0, 0])
     first_leg(2)
-    e_own[...] = dot_nt(slot_by_up, local_t).astype(BF16)
     for d in range(N_SUB):
         mine = dot_nt(query_t, slot_by_up[block(d), :])
         ft[d] = mine
         by_slice_t(fk, d, dot(mine.astype(BF16), spread_t()))
+    serve(3, es[0], pall[0, 1])
+    first_leg(3)
     gather_pass_on(pall, 0, 0)
     gather_start(pall, 1, 0)
-    serve(3, es[0], pall[0, 1])
-    first_leg(3)
     second_leg(2)
     for d in range(1, N_SUB):
         asked_passages(d)
@@ -371,13 +370,21 @@
     )
     used = [jnp.sum(ft[d], axis=0, keepdims=True) for d in range(N_SUB)]
     exp_hard = [jnp.where(used[d] > 0.5, jnp.exp(hard_scores[d : d + 1, :]), 0.0) for d in range(N_SUB)]
+
+    def lanes_for(d, row, start):
+        shape = (N_DP, ROWS)
+        spread_row = jnp.broadcast_to(row.astype(F32), shape)
+        by_row = jnp.where(iota(shape, 0) == iota(shape, 1) // CAP, spread_row, 0.0).astype(BF16)
+        place = one_hot(iota((ROWS, ROWS), 1) == start + d * CAP + iota((ROWS, ROWS), 0) % CAP)
+        return dot(by_row, place)
+
     total = jnp.zeros((ROWS, 1), F32)
     for d in range(N_SUB):
         total += jnp.sum(exp_batch[d] + ft[d] * exp_hard[d], axis=1, keepdims=True)
     diagonal = iota((ROWS, ROWS), 1) == iota((ROWS, ROWS), 0)
     positive = jnp.sum(jnp.where(diagonal, scores[0], 0.0), axis=1, keepdims=True)
     loss_part = jnp.sum(jnp.log(total) - positive, axis=0, keepdims=True)
-    loss_send[...] = jnp.broadcast_to(loss_part, (8, 128))
+    loss_send[...] = jnp.broadcast_to(loss_part, (1, 128))
     for d in range(N_SUB):
         coef = exp_batch[d] / total
         if d == 0:
@@ -386,12 +393,15 @@
         cbm[:, block(d)] = coef.astype(BF16)
         slot_total = jnp.sum(ft[d] * total, axis=0, keepdims=True) + (1.0 - used[d])
         hard_coef = (exp_hard[d] / slot_total).astype(BF16)
-        hard_row = jnp.broadcast_to(hard_coef.astype(F32), (ROWS, ROWS))
-        hard_col = jnp.sum(jnp.where(diagonal, hard_row, 0.0), axis=1, keepdims=True)
-        g_send[block(d), :] = (hard_col * e_own[block(d), :].astype(F32)).astype(BF16)
+        hard_idx = dot_nt(jnp.broadcast_to(loc_row + 1, (8, HARD)).astype(F32).astype(BF16), slot_by_up[block(d), :])
+        g_send[d] = lanes_for((N_SUB - d) % N_SUB, hard_coef, 0) + lanes_for(
+            (N_SUB - d) % N_SUB, hard_idx[0:1, :].astype(BF16), MSG
+        )
         weight = dot(jnp.broadcast_to(hard_coef, (8, ROWS)), spread_t())[0:1, :]
         fk[d] = (fk[d].astype(F32) * weight).astype(BF16)
-    to_mates(g_send, g_recv, 2)
+    for e, mate in mates:
+        send(g_send.at[e], g_recv.at[N_SUB - e], t_s.at[2], t_r.at[2], (dp, mate))
+    g_recv[0] = g_send[0]
     to_mates(cb_send, cb_recv, 3)
 
     def share_loss(dst, index, sem, devices):
@@ -421,21 +431,19 @@
 
     gather_pass_on(qall, 1, 1)
     queries(3)
-    landed(g_recv.at[pl.ds(0, GROUP - ROWS)], t_r.at[2])
-    r = match(N_DP, N_SUB, (SLOTS, SLOTS), 0)
-    c = iota((SLOTS, SLOTS), 1)
-    by_dp = one_hot((c // ROWS == r[1]) & ((c // CAP) % N_DP == r[0]) & (c % CAP == r[2]))
-    w_send[...] = dot(by_dp, g_recv[...]).astype(BF16)
+    landed(g_recv.at[pl.ds(0, N_SUB - 1)], t_r.at[2])
+    w_send[:, 0, :] = g_recv[0] + g_recv[1] + g_recv[2] + g_recv[3]
     to_plane(w_send, w_recv, 5)
     add_loss(loss_z, 4, N_SUB)
     share_loss(loss_x, x, 6, [at(mate, y, core) for mate in mates_x])
+    serve(14, fs[3], qall[3, 1])
+    first_leg(14)
     query_terms(0)
-
-    queries(4)
+    gather_done(qall, 1, 1)
+    serve(15, fs[2], qall[2, 1])
+    first_leg(15)
+    second_leg(13)
     query_terms(1)
-
-    gather_done(qall, 1, 1)
-    queries(5)
     add_loss(loss_x, 6, SIDE)
     share_loss(loss_y, y, 7, [at(x, mate, core) for mate in mates_y])
 
@@ -445,20 +453,26 @@
         for j in range(SLICES):
             pacc[a, block(j), :] = dot(cbt[...], qall[:, a, block(j), :].reshape(GROUP, CW))
 
-    landed(w_recv.at[pl.ds(0, SLOTS - MSG)], t_r.at[5])
-    weights_t = jnp.transpose(w_recv[...].astype(F32)).astype(BF16)
+    second_leg(14)
+    second_leg(15)
+
+    landed(w_recv.at[pl.ds(0, N_DP - 1)], t_r.at[5])
+    by_slot = lax.dot_general(
+        w_recv[:, 0, :].astype(BF16), one_hot(iota((N_DP, SLOTS), 0) == iota((N_DP, SLOTS), 1) // MSG),
+        (((0,), (0,)), ((), ())), preferred_element_type=F32,
+    )
     for d in range(N_SUB):
-        r = match(N_DP, N_SUB, (SLOTS, SLOTS), 0)
-        c = match(N_DP, SLICES, (SLOTS, SLOTS), 1)
-        pick = one_hot((r[0] == c[0]) & (r[2] == c[2]) & (r[1] == d))
-        by_slice_t(es, d, dot(weights_t, pick))
+        lane = iota((ROWS, SLOTS), 0)
+        rank_of = d * CAP + iota((ROWS, SLOTS), 1) % CAP
+        weight = jnp.sum(jnp.where(lane == rank_of, by_slot, 0.0), axis=0, keepdims=True)
+        row = jnp.sum(jnp.where(lane == MSG + rank_of, by_slot, 0.0), axis=0, keepdims=True)
+        by_slice_t(es, d, jnp.where((lane + 1).astype(F32) == row, weight, 0.0))
 
     def passage_terms(n, d, a):
         arrived(n)
         pacc[a] += dot(es[d], rows_of(n))
 
     passage_terms(0, 0, 0)
-    second_leg(15)
     add_loss(loss_y, 7, SIDE)
     share_loss(loss_c, core, 8, [at(x, y, 1 - core)])
     passage_terms(1, 0, 1)
@@ -493,25 +507,25 @@
     lax.fori_loop(3, 6, more_passage_terms, 0)
     stats[1] = jnp.broadcast_to((first + passage_inner(1)) * scale, (ROWS, 128))
 
-    landed(e_send.at[pl.ds(0, SLOTS - MSG)], t_s.at[0])
+    landed(e_send.at[pl.ds(0, N_DP - 1)], t_s.at[0])
     landed(f_send.at[pl.ds(0, GROUP - ROWS)], t_s.at[1])
-    landed(g_send.at[pl.ds(0, GROUP - ROWS)], t_s.at[2])
+    landed(g_send.at[pl.ds(0, N_SUB - 1)], t_s.at[2])
     landed(cb_send.at[pl.ds(0, GROUP - ROWS)], t_s.at[3])
-    landed(w_send.at[pl.ds(0, SLOTS - MSG)], t_s.at[5])
+    landed(w_send.at[pl.ds(0, N_DP - 1)], t_s.at[5])
     landed(pall.at[pl.ds(0, 3)], sent.at[0])
     landed(qall.at[pl.ds(0, 3)], sent.at[1])
     landed(mbuf.at[pl.ds(0, 12)], sent.at[2])
     landed(mbuf.at[pl.ds(0, 14)], sent.at[3])
 
 
-def write_out(loss_in, q_in, pacc, pf, stats, loss_ref, q_hbm, p_hbm, out, sem):
-    copies = [
+def write_out(loss_in, q_in, pacc, pf, stats, loss_hbm, q_hbm, p_hbm, out, loss, sem):
+    loss[...] = loss_in[:, :1]
+    copies = [pltpu.make_async_copy(loss, loss_hbm, sem.at[2, 0])] + [
         pltpu.make_async_copy(q_in.at[pl.ds(i * 32, 32)], q_hbm.at[pl.ds(i * 32, 32)], sem.at[0, i])
         for i in range(4)
     ]
     for copy in copies:
         copy.start()
-    loss_ref[0, 0] = loss_in[0, 0]
     scale = 1.0 / sharpness_divisor
     for i in range(4):
         rows = slice(i * 32, (i + 1) * 32)
@@ -538,7 +552,9 @@
     gathered = pltpu.VMEM((N_SUB, HALVES, GROUP, CW), BF16)
     routed = pltpu.VMEM((ITEMS, 2 * SIDE, SIDE, 2 * MSG, HW), BF16)
     masks = pltpu.VMEM((N_SUB, SLOTS, GROUP), BF16)
-    one_loss = pltpu.VMEM((8, 128), F32)
+    one_loss = pltpu.VMEM((1, 128), F32)
+    plane = pltpu.VMEM((N_DP, 1, 128), F32)
+    mate = pltpu.VMEM((N_SUB, N_DP, 128), F32)
     rows = pltpu.VMEM((ROWS, WIDTH), F32)
     held = pl.pallas_call(
         kernel,
@@ -550,9 +566,9 @@
         scratch_shapes=[
             pltpu.VMEM((1, ROWS), jnp.int32), pltpu.VMEM((1, HARD), jnp.int32), pltpu.VMEM((1, HARD), jnp.int32),
             rows, gathered, gathered, routed, routed, routed,
-            table, table, table, table, table, table, table, table, table, table, table,
-            one_loss, pltpu.VMEM((N_SUB, 8, 128), F32),
-            pltpu.VMEM((SIDE, 8, 128), F32), pltpu.VMEM((SIDE, 8, 128), F32), pltpu.VMEM((2, 8, 128), F32),
+            plane, plane, table, table, table, table, mate, mate, plane, plane,
+            one_loss, pltpu.VMEM((N_SUB, 1, 128), F32),
+            pltpu.VMEM((SIDE, 1, 128), F32), pltpu.VMEM((SIDE, 1, 128), F32), pltpu.VMEM((2, 1, 128), F32),
             pltpu.VMEM((N_SUB, ROWS, ROWS), F32), pltpu.VMEM((8, SLOTS), F32), masks, masks, masks,
             pltpu.VMEM((N_SUB, ROWS, ROWS), F32), pltpu.VMEM((ROWS, GROUP), BF16), pltpu.VMEM((ROWS, GROUP), BF16),
             pltpu.VMEM((ROWS, 128), F32),
@@ -574,8 +590,8 @@
             jax.ShapeDtypeStruct((ROWS, WIDTH), F32),
         ),
         in_specs=[vmem] * 5,
-        out_specs=(pl.BlockSpec(memory_space=pltpu.SMEM), any_space, any_space),
-        scratch_shapes=[rows, dma((2, 4))],
+        out_specs=(any_space,) * 3,
+        scratch_shapes=[rows, pltpu.VMEM((1, 1), F32), dma((3, 4))],
         compiler_params=pltpu.CompilerParams(vmem_limit_bytes=8 * 2**20),
         name="write_out",
     )(*[pltpu.with_memory_space_constraint(v, pltpu.VMEM) for v in held])

time: 110 us -> 104 us (0.945)
  Pallas kernels: 109 us -> 103 us
    pallas_call x1, Pallas kernels: 106 us -> 101 us  [local(): pl.pallas_call(kernel, out_shape=(one_loss, rows, pltpu.VMEM((HALVES, GRO...]
where the time goes in v4:
time: 104 us
  Pallas kernels  103 us (99%)
    pallas_call x1, Pallas kernels, local(): pl.pallas_call(kernel, out_shape=(one_loss, rows, pltpu.VMEM((HALVES, GRO...  101 us
    pallas_call x1, Pallas kernels, local(): pl.pallas_call(write_out, out_shape=(jax.ShapeDtypeStruct((1, 1), F32), j...  2.32 us

profile of v4, /device:TPU:1, one launch (start us, length us, event | category | flops | bytes accessed | tf_op | source)
XLA Modules:
  0.0 104.3 jit_solution(12203482346791404304)
XLA Ops:
  0.6 101.1 %contrastive.1 = (f32[1,128]{1,0:T(1,128)S(1)}, f32[128,4096]{1,0:T(8,128)S(1)}, f32[2,512,512]{2,1,0:T(8,128)S(1)}, f32[128,4096]{1,0:T(8,128)S(1)}, f32[2,128,128]{2,1,0:T(8,128)S(1)}) custom-call(f32[128,4096]{1,0:T(8,128)} %p_hbm.1, f32[128,4096]{1,0:T(8,128)} %q_hbm.1, s32[1,128]{1,0:T(1,128)} %cnt_hbm.1, s32[1,256]{1,0:T(1,128)} %bitcast.2, ...), custom_call_target="tpu_custom_call" | custom-call | tf_op jit(solution)/shard_map/contrastive/pallas_call | solution.py:559
  101.8 2.3 %write_out.1 = (f32[1,1]{1,0:T(1,128)}, f32[128,4096]{1,0:T(8,128)}, f32[128,4096]{1,0:T(8,128)}) custom-call(f32[1,128]{1,0:T(1,128)S(1)} %get-tuple-element.11.loss_in, f32[128,4096]{1,0:T(8,128)S(1)} %get-tuple-element.12.q_in, f32[2,512,512]{2,1,0:T(8,128)S(1)} %get-tuple-element.13.pacc, f32[128,4096]{1,0:T(8,128)S(1)} %get-tuple-element.14.pf, ...), custom_call_target="tpu_custom_call" | custom-call | tf_op jit(solution)/shard_map/write_out/pallas_call | solution.py:585

commit v5 on v4

--- a/solution.py
+++ b/solution.py
@@ -54,13 +54,25 @@
     return slice(j * ROWS, (j + 1) * ROWS)
 
 
+def slot_grads(rows, weights):
+    parts = [rows[:, c : c + 128].astype(F32) * weights for c in range(0, CW, 128)]
+    return jnp.concatenate(parts, axis=1).astype(BF16)
+
+
+def inner_with(pf, inv, grad, a):
+    inner = jnp.zeros((ROWS, 1), F32)
+    for j in range(SLICES):
+        inner += jnp.sum(pf[:, columns(a, j)] * inv * grad[block(j), :], axis=1, keepdims=True)
+    return inner
+
+
 def kernel(
     p_hbm, q_hbm, cnt_hbm, own_hbm, loc_hbm,
-    loss_ref, qg, pacc, pf, stats,
+    loss_ref, qg, pacc, pf, stats, last_rows, last_table, last_weight,
     cnt_ref, own_ref, loc_ref, qf, pall, qall, sbuf, mbuf, rbuf,
     e_send, e_recv, f_send, f_recv, cb_send, cb_recv, g_send, g_recv, w_send, w_recv,
     loss_send, loss_z, loss_x, loss_y, loss_c,
-    sacc, hacc, es, fs, fk, ft, cbm, cbt, qinv,
+    sacc, hacc, es, fs, fk, ft, cbm, cbt, qinv, wcol,
     in_sem, sent, ag_r, a_r, b_r, t_s, t_r,
 ):
     dp = lax.axis_index("dp")
@@ -451,26 +463,32 @@
     cbt[...] = jnp.transpose(cb_recv[...].astype(F32)).astype(BF16)
     for a in range(HALVES):
         for j in range(SLICES):
-            pacc[a, block(j), :] = dot(cbt[...], qall[:, a, block(j), :].reshape(GROUP, CW))
+            pacc[a, block(j), :] = dot(cbt[...], qall[:, a, block(j), :].reshape(GROUP, CW)) * scale
 
     second_leg(14)
     second_leg(15)
 
     landed(w_recv.at[pl.ds(0, N_DP - 1)], t_r.at[5])
-    by_slot = lax.dot_general(
-        w_recv[:, 0, :].astype(BF16), one_hot(iota((N_DP, SLOTS), 0) == iota((N_DP, SLOTS), 1) // MSG),
+    told = w_recv[:, 0, :].astype(BF16)
+    by_slot = dot(one_hot(iota((SLOTS, N_DP), 0) // MSG == iota((SLOTS, N_DP), 1)), told)
+    by_slot_t = lax.dot_general(
+        told, one_hot(iota((N_DP, SLOTS), 0) == iota((N_DP, SLOTS), 1) // MSG),
         (((0,), (0,)), ((), ())), preferred_element_type=F32,
     )
     for d in range(N_SUB):
+        weight_lane = iota((SLOTS, ROWS), 1) == d * CAP + iota((SLOTS, ROWS), 0) % CAP
+        weight = jnp.sum(jnp.where(weight_lane, by_slot, 0.0), axis=1, keepdims=True)
+        wcol[d] = jnp.broadcast_to(weight * scale, (SLOTS, 128))
         lane = iota((ROWS, SLOTS), 0)
-        rank_of = d * CAP + iota((ROWS, SLOTS), 1) % CAP
-        weight = jnp.sum(jnp.where(lane == rank_of, by_slot, 0.0), axis=0, keepdims=True)
-        row = jnp.sum(jnp.where(lane == MSG + rank_of, by_slot, 0.0), axis=0, keepdims=True)
-        by_slice_t(es, d, jnp.where((lane + 1).astype(F32) == row, weight, 0.0))
+        row_lane = lane == MSG + d * CAP + iota((ROWS, SLOTS), 1) % CAP
+        row = jnp.sum(jnp.where(row_lane, by_slot_t, 0.0), axis=0, keepdims=True)
+        by_slice_t(es, d, one_hot((lane + 1).astype(F32) == row))
+    last_table[...] = es[2]
+    last_weight[...] = wcol[2]
 
     def passage_terms(n, d, a):
         arrived(n)
-        pacc[a] += dot(es[d], rows_of(n))
+        pacc[a] += dot(es[d], slot_grads(rows_of(n), wcol[d]))
 
     passage_terms(0, 0, 0)
     add_loss(loss_y, 7, SIDE)
@@ -494,18 +512,14 @@
 
     inv = stats[0, :, :1]
 
-    def passage_inner(a):
-        inner = jnp.zeros((ROWS, 1), F32)
-        for j in range(SLICES):
-            inner += jnp.sum(pf[:, columns(a, j)] * inv * pacc[a, block(j), :], axis=1, keepdims=True)
-        return inner
-
     lax.fori_loop(0, 3, more_passage_terms, 0)
-    first = passage_inner(0)
+    first = inner_with(pf, inv, pacc.at[0], 0)
     add_loss(loss_c, 8, 2)
     loss_ref[...] = loss_send[...] / (ROWS * N_DP * N_SUB)
-    lax.fori_loop(3, 6, more_passage_terms, 0)
-    stats[1] = jnp.broadcast_to((first + passage_inner(1)) * scale, (ROWS, 128))
+    stats[1] = jnp.broadcast_to(first, (ROWS, 128))
+    lax.fori_loop(3, 5, more_passage_terms, 0)
+    arrived(15)
+    last_rows[...] = rows_of(15)
 
     landed(e_send.at[pl.ds(0, N_DP - 1)], t_s.at[0])
     landed(f_send.at[pl.ds(0, GROUP - ROWS)], t_s.at[1])
@@ -518,7 +532,11 @@
     landed(mbuf.at[pl.ds(0, 14)], sent.at[3])
 
 
-def write_out(loss_in, q_in, pacc, pf, stats, loss_hbm, q_hbm, p_hbm, out, loss, sem):
+def write_out(
+    loss_in, q_in, pacc, pf, stats, last_rows, last_table, last_weight,
+    loss_hbm, q_hbm, p_hbm,
+    out, grad, loss, sem,
+):
     loss[...] = loss_in[:, :1]
     copies = [pltpu.make_async_copy(loss, loss_hbm, sem.at[2, 0])] + [
         pltpu.make_async_copy(q_in.at[pl.ds(i * 32, 32)], q_hbm.at[pl.ds(i * 32, 32)], sem.at[0, i])
@@ -526,16 +544,18 @@
     ]
     for copy in copies:
         copy.start()
-    scale = 1.0 / sharpness_divisor
+    grad[...] = pacc[1] + dot(last_table[...], slot_grads(last_rows[...], last_weight[...]))
+    inners = stats[1, :, :1] + inner_with(pf, stats[0, :, :1], grad, 1)
     for i in range(4):
         rows = slice(i * 32, (i + 1) * 32)
         inv = stats[0, rows, :1]
-        inner = stats[1, rows, :1]
-        for a in range(HALVES):
-            for j in range(SLICES):
-                cols = columns(a, j)
-                grad = pacc[a, j * ROWS + i * 32 : j * ROWS + (i + 1) * 32, :] * scale
-                out[rows, cols] = (grad - pf[rows, cols] * inv * inner) * inv
+        inner = inners[rows, :]
+        for j in range(SLICES):
+            part = slice(j * ROWS + i * 32, j * ROWS + (i + 1) * 32)
+            cols = columns(0, j)
+            out[rows, cols] = (pacc[0, part, :] - pf[rows, cols] * inv * inner) * inv
+            cols = columns(1, j)
+            out[rows, cols] = (grad[part, :] - pf[rows, cols] * inv * inner) * inv
         copy = pltpu.make_async_copy(out.at[pl.ds(i * 32, 32)], p_hbm.at[pl.ds(i * 32, 32)], sem.at[1, i])
         copy.start()
         copies.append(copy)
@@ -560,9 +580,10 @@
         kernel,
         out_shape=(
             one_loss, rows, pltpu.VMEM((HALVES, GROUP, CW), F32), rows, pltpu.VMEM((2, ROWS, 128), F32),
+            pltpu.VMEM((SLOTS, CW), BF16), pltpu.VMEM((GROUP, SLOTS), BF16), pltpu.VMEM((SLOTS, 128), F32),
         ),
         in_specs=[hbm] * 5,
-        out_specs=(vmem,) * 5,
+        out_specs=(vmem,) * 8,
         scratch_shapes=[
             pltpu.VMEM((1, ROWS), jnp.int32), pltpu.VMEM((1, HARD), jnp.int32), pltpu.VMEM((1, HARD), jnp.int32),
             rows, gathered, gathered, routed, routed, routed,
@@ -571,11 +592,11 @@
             pltpu.VMEM((SIDE, 1, 128), F32), pltpu.VMEM((SIDE, 1, 128), F32), pltpu.VMEM((2, 1, 128), F32),
             pltpu.VMEM((N_SUB, ROWS, ROWS), F32), pltpu.VMEM((8, SLOTS), F32), masks, masks, masks,
             pltpu.VMEM((N_SUB, ROWS, ROWS), F32), pltpu.VMEM((ROWS, GROUP), BF16), pltpu.VMEM((ROWS, GROUP), BF16),
-            pltpu.VMEM((ROWS, 128), F32),
+            pltpu.VMEM((ROWS, 128), F32), pltpu.VMEM((N_SUB, SLOTS, 128), F32),
             dma((5,)), dma((4,)), dma((2, HALVES, 3)), dma((ITEMS,)), dma((ITEMS,)), dma((9,)), dma((9,)),
         ],
         compiler_params=pltpu.CompilerParams(
-            collective_id=0, has_side_effects=True, vmem_limit_bytes=53 * 2**20
+            collective_id=0, has_side_effects=True, vmem_limit_bytes=51 * 2**20
         ),
         name="contrastive",
     )(*[
@@ -589,10 +610,10 @@
             jax.ShapeDtypeStruct((ROWS, WIDTH), F32),
             jax.ShapeDtypeStruct((ROWS, WIDTH), F32),
         ),
-        in_specs=[vmem] * 5,
+        in_specs=[vmem] * 8,
         out_specs=(any_space,) * 3,
-        scratch_shapes=[rows, pltpu.VMEM((1, 1), F32), dma((3, 4))],
-        compiler_params=pltpu.CompilerParams(vmem_limit_bytes=8 * 2**20),
+        scratch_shapes=[rows, pltpu.VMEM((GROUP, CW), F32), pltpu.VMEM((1, 1), F32), dma((3, 4))],
+        compiler_params=pltpu.CompilerParams(vmem_limit_bytes=10 * 2**20),
         name="write_out",
     )(*[pltpu.with_memory_space_constraint(v, pltpu.VMEM) for v in held])
     return loss.reshape(()), query_grad, passage_grad

time: 104 us -> 104 us (level)
  no operation moved by 1% of the time
where the time goes in v5:
time: 104 us
  Pallas kernels  103 us (99%)
    pallas_call x1, Pallas kernels, local(): pl.pallas_call(kernel, out_shape=(one_loss, rows, pltpu.VMEM((HALVES, GRO...  101 us
    pallas_call x1, Pallas kernels, local(): pl.pallas_call(write_out, out_shape=(jax.ShapeDtypeStruct((1, 1), F32), j...  2.71 us

profile of v5, /device:TPU:1, one launch (start us, length us, event | category | flops | bytes accessed | tf_op | source)
XLA Modules:
  0.0 104.1 jit_solution(1648272554790676775)
XLA Ops:
  0.6 100.6 %contrastive.1 = (f32[1,128]{1,0:T(1,128)S(1)}, f32[128,4096]{1,0:T(8,128)S(1)}, f32[2,512,512]{2,1,0:T(8,128)S(1)}, f32[128,4096]{1,0:T(8,128)S(1)}, f32[2,128,...) custom-call(f32[128,4096]{1,0:T(8,128)} %p_hbm.1, ...), custom_call_target="tpu_custom_call" | custom-call | tf_op jit(solution)/shard_map/contrastive/pallas_call | solution.py:579
  101.2 2.7 %write_out.1 = (f32[1,1]{1,0:T(1,128)}, f32[128,4096]{1,0:T(8,128)}, f32[128,4096]{1,0:T(8,128)}) custom-call(f32[1,128]{1,0:T(1,128)S(1)} %get-tuple-element.14.loss_in, f32[128,4096]{1,0:T(8,128)S(1)} %get-tuple-element.15.q_in, f32[2,512,512]{2,1,0:T(8,128)S(1)} %get-tuple-element.16.pacc, f32[128,4096]{1,0:T(8,128)S(1)} %get-tuple-element.17.pf, ...), custom_call_target="tpu_custom_call" | custom-call | tf_op jit(solution)/shard_map/write_out/pallas_call | solution.py:606

commit v6 on v5

--- a/solution.py
+++ b/solution.py
@@ -134,8 +134,10 @@
         dst[block(0), :] = src[block(0), :]
 
     def gather_start(buf, a, which):
-        send(buf.at[0, a], buf.at[3, a], sent.at[which], ag_r.at[which, a, 0], (dp, above))
-        send(buf.at[0, a], buf.at[1, a], sent.at[which], ag_r.at[which, a, 1], (dp, below))
+        for i in range(4):
+            part = pl.ds(i * ROWS, ROWS)
+            send(buf.at[0, a, part], buf.at[3, a, part], sent.at[which], ag_r.at[which, a, 0], (dp, above))
+            send(buf.at[0, a, part], buf.at[1, a, part], sent.at[which], ag_r.at[which, a, 1], (dp, below))
 
     def gather_pass_on(buf, a, which):
         landed(buf.at[3, a], ag_r.at[which, a, 0])
@@ -254,14 +256,14 @@
     with jax.named_scope("entry_barrier"):
         pl.semaphore_wait(barrier, N_DP - 1 + N_SUB - 1)
     first_leg(0)
+    with jax.named_scope("passages_in"):
+        p_in.wait()
+    stats[0] = normalize(pf, pall)
+    gather_start(pall, 0, 0)
     asks = one_hot(iota((N_DP, HARD), 0) == owner_dp)
     row_at = jnp.where(iota((ROWS, HARD), 0) == up * CAP + rank, loc_row + 1, 0).astype(F32).astype(BF16)
     e_send[:, 0, :] = dot_nt(asks, row_at)
     to_plane(e_send, e_recv, 0)
-    with jax.named_scope("passages_in"):
-        p_in.wait()
-    stats[0] = normalize(pf, pall)
-    gather_start(pall, 0, 0)
     serve(1, fs[0], qall[0, 1])
     first_leg(1)
     slot_by_up = one_hot(iota((SLOTS, HARD), 0) == up * ROWS + owner_dp * CAP + rank)

time: 104 us -> 104 us (level)
  no operation moved by 1% of the time
where the time goes in v6:
time: 104 us
  Pallas kernels  103 us (99%)
    pallas_call x1, Pallas kernels, local(): pl.pallas_call(kernel, out_shape=(one_loss, rows, pltpu.VMEM((HALVES, GRO...  101 us
    pallas_call x1, Pallas kernels, local(): pl.pallas_call(write_out, out_shape=(jax.ShapeDtypeStruct((1, 1), F32), j...  2.71 us

profile of v6, /device:TPU:1, one launch (start us, length us, event | category | flops | bytes accessed | tf_op | source)
XLA Modules:
  0.0 104.0 jit_solution(12899476894983635474)
XLA Ops:
  0.6 100.5 %contrastive.1 = (f32[1,128]{1,0:T(1,128)S(1)}, f32[128,4096]{1,0:T(8,128)S(1)}, f32[2,512,512]{2,1,0:T(8,128)S(1)}, f32[128,4096]{1,0:T(8,128)S(1)}, f32[2,128,...) custom-call(f32[128,4096]{1,0:T(8,128)} %p_hbm.1, ...), custom_call_target="tpu_custom_call" | custom-call | tf_op jit(solution)/shard_map/contrastive/pallas_call | solution.py:581
  101.2 2.7 %write_out.1 = (f32[1,1]{1,0:T(1,128)}, f32[128,4096]{1,0:T(8,128)}, f32[128,4096]{1,0:T(8,128)}) custom-call(f32[1,128]{1,0:T(1,128)S(1)} %get-tuple-element.14.loss_in, f32[128,4096]{1,0:T(8,128)S(1)} %get-tuple-element.15.q_in, f32[2,512,512]{2,1,0:T(8,128)S(1)} %get-tuple-element.16.pacc, f32[128,4096]{1,0:T(8,128)S(1)} %get-tuple-element.17.pf, ...), custom_call_target="tpu_custom_call" | custom-call | tf_op jit(solution)/shard_map/write_out/pallas_call | solution.py:608

commit v7 on v6

--- a/solution.py
+++ b/solution.py
@@ -516,10 +516,10 @@
 
     lax.fori_loop(0, 3, more_passage_terms, 0)
     first = inner_with(pf, inv, pacc.at[0], 0)
+    stats[1] = jnp.broadcast_to(first, (ROWS, 128))
+    lax.fori_loop(3, 5, more_passage_terms, 0)
     add_loss(loss_c, 8, 2)
     loss_ref[...] = loss_send[...] / (ROWS * N_DP * N_SUB)
-    stats[1] = jnp.broadcast_to(first, (ROWS, 128))
-    lax.fori_loop(3, 5, more_passage_terms, 0)
     arrived(15)
     last_rows[...] = rows_of(15)
 

time: 104 us -> 104 us (level)
  no operation moved by 1% of the time
where the time goes in v7:
time: 104 us
  Pallas kernels  103 us (99%)
    pallas_call x1, Pallas kernels, local(): pl.pallas_call(kernel, out_shape=(one_loss, rows, pltpu.VMEM((HALVES, GRO...  101 us
    pallas_call x1, Pallas kernels, local(): pl.pallas_call(write_out, out_shape=(jax.ShapeDtypeStruct((1, 1), F32), j...  2.71 us

profile of v7, /device:TPU:1, one launch (start us, length us, event | category | flops | bytes accessed | tf_op | source)
XLA Modules:
  0.0 104.0 jit_solution(6714618500844012052)
XLA Ops:
  0.6 100.5 %contrastive.1 = (f32[1,128]{1,0:T(1,128)S(1)}, f32[128,4096]{1,0:T(8,128)S(1)}, f32[2,512,512]{2,1,0:T(8,128)S(1)}, f32[128,4096]{1,0:T(8,128)S(1)}, f32[2,128,...) custom-call(f32[128,4096]{1,0:T(8,128)} %p_hbm.1, ...), custom_call_target="tpu_custom_call" | custom-call | tf_op jit(solution)/shard_map/contrastive/pallas_call | solution.py:581
  101.2 2.7 %write_out.1 = (f32[1,1]{1,0:T(1,128)}, f32[128,4096]{1,0:T(8,128)}, f32[128,4096]{1,0:T(8,128)}) custom-call(f32[1,128]{1,0:T(1,128)S(1)} %get-tuple-element.14.loss_in, f32[128,4096]{1,0:T(8,128)S(1)} %get-tuple-element.15.q_in, f32[2,512,512]{2,1,0:T(8,128)S(1)} %get-tuple-element.16.pacc, f32[128,4096]{1,0:T(8,128)S(1)} %get-tuple-element.17.pf, ...), custom_call_target="tpu_custom_call" | custom-call | tf_op jit(solution)/shard_map/write_out/pallas_call | solution.py:608
